TPU v7x, 512 devices: a whole 4x4x16 slice. The times are simulated.
512 devices in a mesh: lat: 64 (over x, z_lo, core), tp: 8 (over z_hi, y).
Axes of the slice: x: 4, y: 4, z: 16 (z_hi: 2, z_lo: 8; z = z_hi * 8 + z_lo), core: 2. Of those that a mesh axis runs over, the one named last changes fastest.
Arguments:
- fields: bfloat16 [128, 4, 64, 512], P('lat'), may hold values from -16 to 16
- classes: int32 [128, 64], P('lat'), may hold values from 0 to 7
- class_table: bfloat16 [8, 512], replicated, may hold values from -4 to 4
- gain_fine: float32 [512], replicated, may hold values from 0.1 to 1.9
- fine_qkv: bfloat16 [512, 8, 192], P(None, 'tp'), may hold values from -1.5 to 1.5
- fine_out: bfloat16 [8, 64, 512], P('tp'), may hold values from -0.25 to 0.25
- gain_merge: float32 [2048], replicated, may hold values from 0.1 to 1.9
- merge_weight: bfloat16 [2048, 1024], P(None, 'tp'), may hold values from -0.125 to 0.125
- gain_coarse: float32 [1024], replicated, may hold values from 0.1 to 1.9
- coarse_qkv: bfloat16 [1024, 16, 192], P(None, 'tp'), may hold values from -1.5 to 1.5
- coarse_out: bfloat16 [16, 64, 1024], P('tp'), may hold values from -0.1875 to 0.1875
- up_weight: bfloat16 [1024, 2048], P(None, 'tp'), may hold values from -0.1875 to 0.1875
- cotangent: bfloat16 [128, 4, 64, 512], P('lat'), may hold values from -6 to 6
Outputs:
- next_fields: bfloat16 [128, 4, 64, 512], P('lat')
- fields_grad: bfloat16 [128, 4, 64, 512], P('lat', None, 'tp')
- fine_qkv_grad: float32 [512, 8, 192], P('lat', 'tp')
- merge_weight_grad: float32 [2048, 1024], P('lat', 'tp')
All inputs are finite; a program needn't handle non-finite values.
Results may differ from a plain program's by a relative error of at most 0.035.
Values may be sent and summed in bfloat16 or wider, within the bound.
A program may use at most 64 MiB of HBM per device.

v0:
```python
import jax
import jax.numpy as jnp
from jax import lax
from jax.sharding import PartitionSpec as P

WIN = 8


EPSILON = 1e-05
NEGATIVE = -1e30


def extended(x, sides, width):
    for axis, dim in sides:
        size, length = (lax.axis_size(axis), x.shape[dim])
        up = [(i, (i + 1) % size) for i in range(size - 1)]
        down = [(j, i) for i, j in up]
        last = lax.slice_in_dim(x, length - width, length, axis=dim)
        initial = lax.slice_in_dim(x, 0, width, axis=dim)
        before = lax.ppermute(last, axis, up)
        after = lax.ppermute(initial, axis, down)
        x = jnp.concatenate([before, x, after], axis=dim)
    return x


def partner(x, axis, distance):
    return lax.ppermute(x, axis, [(i, i ^ 1 << distance) for i in range(lax.axis_size(axis))])


def normalize(values, gain_vector):
    average = jnp.mean(values, axis=-1, keepdims=True)
    centred = values - average
    spread = jnp.mean(centred * centred, axis=-1, keepdims=True)
    return centred * lax.rsqrt(spread + EPSILON) * gain_vector


def normalize_back(values, gain_vector, incoming):
    return jax.vjp(lambda argument: normalize(argument, gain_vector), values)[1](incoming)[0]


def contract(pattern, operand_a, operand_b):
    return jnp.einsum(pattern, operand_a, operand_b, preferred_element_type=jnp.float32)


def widen_keys(kv_term, head_size):
    return jnp.concatenate([jnp.zeros_like(kv_term[..., :head_size]), kv_term], axis=-1)


def to_windows(values, offset, window_width):
    row_count, levels, lon_count, head_count, head_depth = values.shape
    rolled = jnp.roll(values, -offset, axis=2)
    grouped = rolled.reshape(
        row_count, levels, lon_count // window_width, window_width, head_count, head_depth
    )
    grouped = grouped.transpose(0, 2, 4, 1, 3, 5)
    return grouped.reshape(
        row_count, lon_count // window_width, head_count, levels * window_width, head_depth
    )


def from_windows(values, offset, levels):
    row_count, window_count, head_count, window_tokens, head_depth = values.shape
    window_width = window_tokens // levels
    grouped = values.reshape(row_count, window_count, head_count, levels, window_width, head_depth)
    grouped = grouped.transpose(0, 3, 1, 4, 2, 5)
    joined = grouped.reshape(row_count, levels, window_count * window_width, head_count, head_depth)
    return jnp.roll(joined, offset, axis=2)


def pack_quads(values):
    row_count, levels, lon_count, feature_width = values.shape
    grouped = values.reshape(row_count // 2, 2, levels, lon_count // 2, 2, feature_width)
    return grouped.transpose(0, 2, 3, 1, 4, 5).reshape(
        row_count // 2, levels, lon_count // 2, 4 * feature_width
    )


def unpack_quads(values):
    row_count, levels, lon_count, packed_width = values.shape
    grouped = values.reshape(row_count, levels, lon_count, 2, 2, packed_width // 4)
    return grouped.transpose(0, 3, 1, 2, 4, 5).reshape(
        2 * row_count, levels, 2 * lon_count, packed_width // 4
    )


def window_attend(queries, key_own, value_own, key_partner, value_partner, present, score_scale):
    score_own = contract("rwhqe,rwhke->rwhqk", queries, key_own) * score_scale
    score_partner = contract("rwhqe,rwhke->rwhqk", queries, key_partner) * score_scale
    score_partner = jnp.where(present, score_partner, NEGATIVE)
    largest = jnp.maximum(
        jnp.max(score_own, axis=-1, keepdims=True), jnp.max(score_partner, axis=-1, keepdims=True)
    )
    exp_own = jnp.exp(score_own - largest)
    exp_partner = jnp.exp(score_partner - largest)
    denominator = jnp.sum(exp_own, axis=-1, keepdims=True) + jnp.sum(
        exp_partner, axis=-1, keepdims=True
    )
    prob_own = exp_own / denominator
    prob_partner = exp_partner / denominator
    mixture = contract("rwhqk,rwhke->rwhqe", prob_own.astype(jnp.bfloat16), value_own)
    mixture = mixture + contract(
        "rwhqk,rwhke->rwhqe", prob_partner.astype(jnp.bfloat16), value_partner
    )
    return (mixture.astype(jnp.bfloat16), prob_own, prob_partner)


def window_back(
    queries,
    key_own,
    value_own,
    key_partner,
    value_partner,
    prob_own,
    prob_partner,
    grad_out,
    score_scale,
):
    half_own = prob_own.astype(jnp.bfloat16)
    half_partner = prob_partner.astype(jnp.bfloat16)
    value_grad_own = contract("rwhqk,rwhqe->rwhke", half_own, grad_out)
    value_grad_partner = contract("rwhqk,rwhqe->rwhke", half_partner, grad_out)
    prob_grad_own = contract("rwhqe,rwhke->rwhqk", grad_out, value_own)
    prob_grad_partner = contract("rwhqe,rwhke->rwhqk", grad_out, value_partner)
    row_dot = jnp.sum(prob_grad_own * prob_own, axis=-1, keepdims=True)
    row_dot = row_dot + jnp.sum(prob_grad_partner * prob_partner, axis=-1, keepdims=True)
    score_grad_own = (prob_own * (prob_grad_own - row_dot) * score_scale).astype(jnp.bfloat16)
    score_grad_partner = (prob_partner * (prob_grad_partner - row_dot) * score_scale).astype(
        jnp.bfloat16
    )
    query_grad = contract("rwhqk,rwhke->rwhqe", score_grad_own, key_own)
    query_grad = query_grad + contract("rwhqk,rwhke->rwhqe", score_grad_partner, key_partner)
    key_grad_own = contract("rwhqk,rwhqe->rwhke", score_grad_own, queries)
    key_grad_partner = contract("rwhqk,rwhqe->rwhke", score_grad_partner, queries)
    return (query_grad, key_grad_own, value_grad_own, key_grad_partner, value_grad_partner)


def local(
    fields,
    classes,
    class_table,
    gain_fine,
    fine_qkv,
    fine_out,
    gain_merge,
    merge_weight,
    gain_coarse,
    coarse_qkv,
    coarse_out,
    up_weight,
    cotangent,
):
    row_count, levels, lon_count, feature_width = fields.shape
    head_size = fine_qkv.shape[2] // 3
    coarse_head = coarse_qkv.shape[2] // 3
    lat_count = lax.axis_size("lat")
    lat_index = lax.axis_index("lat")
    tp_count = lax.axis_size("tp")
    tp_index = lax.axis_index("tp")
    norm_scale = (row_count * lat_count * levels * lon_count) ** (-0.5)
    offset = WIN // 2
    lon_share = lon_count // tp_count
    class_count = class_table.shape[0]
    onehot = (classes[..., None] == jnp.arange(class_count, dtype=jnp.int32)).astype(jnp.bfloat16)
    embedded = jnp.dot(
        onehot.reshape(-1, class_count), class_table, preferred_element_type=jnp.float32
    )
    hidden = fields.astype(jnp.float32) + embedded.reshape(row_count, 1, lon_count, feature_width)
    hidden_share = lax.dynamic_slice_in_dim(hidden, tp_index * lon_share, lon_share, 2)
    normed = normalize(hidden, gain_fine).astype(jnp.bfloat16)
    present = jnp.stack([lat_index > 0, lat_index < lat_count - 1]).reshape(2, 1, 1, 1, 1)
    padded = extended(normed, (("lat", 0),), 1)
    projected = contract("tvxd,dhe->tvxhe", padded, fine_qkv).astype(jnp.bfloat16)
    qkv = projected[1:3]
    rim_kv = jnp.concatenate([projected[0:1], projected[3:4]], axis=0)[..., head_size:]
    rim_rows = jnp.concatenate([padded[0:1], padded[3:4]], axis=0)
    queries = to_windows(qkv[..., :head_size], offset, WIN)
    key_own = to_windows(qkv[..., head_size : 2 * head_size], offset, WIN)
    value_own = to_windows(qkv[..., 2 * head_size :], offset, WIN)
    key_partner = to_windows(rim_kv[..., :head_size], offset, WIN)
    value_partner = to_windows(rim_kv[..., head_size:], offset, WIN)
    score_scale = head_size ** (-0.5)
    mixture, prob_own, prob_partner = window_attend(
        queries, key_own, value_own, key_partner, value_partner, present, score_scale
    )
    fine_heads = from_windows(mixture, offset, levels)
    partial_out = contract("tvxhe,hed->tvxd", fine_heads, fine_out)
    resid = hidden + lax.psum(partial_out, "tp")
    merged = pack_quads(resid)
    merged_norm = normalize(merged, gain_merge).astype(jnp.bfloat16)
    coarse_part = contract("tvxm,mc->tvxc", merged_norm, merge_weight).astype(jnp.bfloat16)
    coarse = lax.all_gather(coarse_part, "tp", axis=3, tiled=True)
    coarse_wide = coarse.astype(jnp.float32)
    coarse_norm = normalize(coarse_wide, gain_coarse).astype(jnp.bfloat16)
    cqkv = contract("tvxc,che->tvxhe", coarse_norm, coarse_qkv).astype(jnp.bfloat16)
    partner_kv = partner(cqkv[..., coarse_head:], "lat", 0)
    coarse_queries = to_windows(cqkv[..., :coarse_head], 0, WIN)
    coarse_keys = to_windows(cqkv[..., coarse_head : 2 * coarse_head], 0, WIN)
    coarse_values = to_windows(cqkv[..., 2 * coarse_head :], 0, WIN)
    partner_keys = to_windows(partner_kv[..., :coarse_head], 0, WIN)
    partner_values = to_windows(partner_kv[..., coarse_head:], 0, WIN)
    coarse_scale = coarse_head ** (-0.5)
    coarse_mix, coarse_own, coarse_other = window_attend(
        coarse_queries, coarse_keys, coarse_values, partner_keys, partner_values, True, coarse_scale
    )
    coarse_heads = from_windows(coarse_mix, 0, levels)
    coarse_sum = lax.psum(
        contract("tvxhe,hec->tvxc", coarse_heads, coarse_out).astype(jnp.bfloat16), "tp"
    ).astype(jnp.float32)
    lifted = (coarse_wide + coarse_sum).astype(jnp.bfloat16)
    up_part = contract("tvxc,cu->tvxu", lifted, up_weight).astype(jnp.bfloat16)
    upsampled = lax.all_gather(up_part, "tp", axis=3, tiled=True)
    next_fields = (resid + unpack_quads(upsampled).astype(jnp.float32)).astype(jnp.bfloat16)
    grad_up = pack_quads(cotangent)
    up_columns = up_weight.shape[1]
    grad_up_own = lax.dynamic_slice_in_dim(grad_up, tp_index * up_columns, up_columns, 3)
    lift_sum = lax.psum(
        contract("tvxu,cu->tvxc", grad_up_own, up_weight).astype(jnp.bfloat16), "tp"
    )
    grad_cheads = contract("tvxc,hec->tvxhe", lift_sum, coarse_out).astype(jnp.bfloat16)
    coarse_terms = window_back(
        coarse_queries,
        coarse_keys,
        coarse_values,
        partner_keys,
        partner_values,
        coarse_own,
        coarse_other,
        to_windows(grad_cheads, 0, WIN),
        coarse_scale,
    )
    grad_cqkv = from_windows(jnp.concatenate(coarse_terms[:3], axis=-1), 0, levels).astype(
        jnp.bfloat16
    )
    grad_ckv = from_windows(jnp.concatenate(coarse_terms[3:], axis=-1), 0, levels).astype(
        jnp.bfloat16
    )
    returned_ckv = partner(grad_ckv, "lat", 0)
    partial_cnorm = contract("tvxhe,che->tvxc", grad_cqkv, coarse_qkv)
    partial_cnorm = partial_cnorm + contract(
        "tvxhe,che->tvxc", returned_ckv, coarse_qkv[..., coarse_head:]
    )
    grad_cnorm = lax.psum(partial_cnorm.astype(jnp.bfloat16), "tp").astype(jnp.float32)
    grad_coarse = (
        lift_sum.astype(jnp.float32) + normalize_back(coarse_wide, gain_coarse, grad_cnorm)
    ).astype(jnp.bfloat16)
    merge_columns = merge_weight.shape[1]
    grad_coarse_own = lax.dynamic_slice_in_dim(
        grad_coarse, tp_index * merge_columns, merge_columns, 3
    )
    merge_term = contract("tvxm,tvxc->mc", merged_norm, grad_coarse_own) * norm_scale
    merge_weight_grad = lax.psum_scatter(merge_term, "lat", scatter_dimension=0, tiled=True)
    grad_mnorm = lax.psum(
        contract("tvxc,mc->tvxm", grad_coarse_own, merge_weight).astype(jnp.bfloat16), "tp"
    ).astype(jnp.float32)
    grad_merged = normalize_back(merged, gain_merge, grad_mnorm)
    grad_resid = (cotangent.astype(jnp.float32) + unpack_quads(grad_merged)).astype(jnp.bfloat16)
    resid_share = lax.dynamic_slice_in_dim(grad_resid, tp_index * lon_share, lon_share, 2)
    grad_heads = contract("tvxd,hed->tvxhe", grad_resid, fine_out).astype(jnp.bfloat16)
    fine_terms = window_back(
        queries,
        key_own,
        value_own,
        key_partner,
        value_partner,
        prob_own,
        prob_partner,
        to_windows(grad_heads, offset, WIN),
        score_scale,
    )
    grad_qkv = from_windows(jnp.concatenate(fine_terms[:3], axis=-1), offset, levels).astype(
        jnp.bfloat16
    )
    grad_kv = from_windows(jnp.concatenate(fine_terms[3:], axis=-1), offset, levels).astype(
        jnp.bfloat16
    )
    kv_weight = fine_qkv[..., head_size:]
    own_norm = contract("tvxhe,dhe->tvxd", grad_qkv, fine_qkv)
    own_weight = contract("tvxd,tvxhe->dhe", normed, grad_qkv)
    rim_grad = contract("tvxhe,dhe->tvxd", grad_kv, kv_weight)
    returned_rows = extended(rim_grad.astype(jnp.bfloat16), (("lat", 0),), 1).astype(rim_grad.dtype)
    partial_norm = own_norm + jnp.concatenate([returned_rows[0:1], returned_rows[3:4]], axis=0)
    partial_weight = own_weight + widen_keys(
        contract("tvxd,tvxhe->dhe", rim_rows, grad_kv), head_size
    )
    grad_norm = lax.psum_scatter(
        partial_norm.astype(jnp.bfloat16), "tp", scatter_dimension=2, tiled=True
    ).astype(jnp.float32)
    fields_grad = (
        resid_share.astype(jnp.float32) + normalize_back(hidden_share, gain_fine, grad_norm)
    ).astype(jnp.bfloat16)
    fine_qkv_grad = lax.psum_scatter(
        partial_weight * norm_scale, "lat", scatter_dimension=0, tiled=True
    )
    return (next_fields, fields_grad, fine_qkv_grad, merge_weight_grad)


def solution(mesh):
    placed = (
        P("lat", None, None, None),
        P("lat", None),
        P(),
        P(),
        P(None, "tp", None),
        P("tp", None, None),
        P(),
        P(None, "tp"),
        P(),
        P(None, "tp", None),
        P("tp", None, None),
        P(None, "tp"),
        P("lat", None, None, None),
    )
    return jax.shard_map(
        local,
        mesh=mesh,
        in_specs=placed,
        out_specs=(
            P("lat", None, None, None),
            P("lat", None, "tp", None),
            P("lat", "tp", None),
            P("lat", "tp"),
        ),
        check_vma=False,
    )
```

profile of v0, /device:TPU:1, one launch (start us, length us, event | category | flops | bytes accessed | tf_op | source)
XLA Modules:
  0.0 2146.0 jit_solution(17858095765121194177)
XLA Ops:
  7.2 1.0 fusion.186
  8.2 2.2 convert_add_fusion
  12.5 4.9 collective-permute-start
  17.4 5.8 collective-permute-start.1
  24.9 1.0 fusion.6
  26.9 1.5 convolution_convert_fusion.1
  32.2 1.2 fusion.83
  33.5 146.5 %all-reduce.11.cloned.1.call-done = bf16[1,4,32,1024]{3,2,1,0:T(8,128)(2,1)} async-done(((bf16[1,4,32,1024]{3,2,1,0:T(8,128)(2,1)}), bf16[1,4,32,1024]{3,2,1,0:T(8,128)(2,1)}) %all-reduce.11.cloned.1.call-update) | async-done | bytes 262160 | tf_op jit(solution)/shard_map/psum | solution.py:216
  180.0 1.9 fusion.22
  181.9 167.6 %all-reduce.9.cloned.1.call-done = f32[2,4,64,512]{3,2,1,0:T(8,128)} async-done(((f32[2,4,64,512]{3,2,1,0:T(8,128)}), f32[2,4,64,512]{3,2,1,0:T(8,128)}) %all-reduce.9.cloned.1.call-update) | async-done | bytes 1048592 | tf_op jit(solution)/shard_map/psum | solution.py:187
  349.5 1.4 fusion.29
  354.2 1.9 reshape.740
  356.2 1.6 convolution_convert_fusion.12
  357.7 55.5 %all-gather = bf16[4,32,1024]{2,1,0:T(8,128)(2,1)S(1)} all-gather(bf16[4,32,128]{2,1,0:T(8,128)(2,1)S(1)} %convolution_convert_fusion.12), channel_id=2, replica_groups=mesh['lat'=64,'tp'=8] {'tp'}, dimensions={2}, use_global_device_ids=true | all-gather | bytes 294912 | tf_op jit(solution)/shard_map/all_gather | solution.py:191
  415.1 9.7 collective-permute-start.2
  428.5 2.3 collective-permute-start.3
  434.7 143.7 %all-reduce.13.cloned.1.call-done = bf16[1,4,32,1024]{3,2,1,0:T(8,128)(2,1)} async-done(((bf16[1,4,32,1024]{3,2,1,0:T(8,128)(2,1)}), bf16[1,4,32,1024]{3,2,1,0:T(8,128)(2,1)}) %all-reduce.13.cloned.1.call-update) | async-done | bytes 262160 | tf_op jit(solution)/shard_map/psum | solution.py:242
  578.4 1.2 fusion.42
  580.7 1.9 fusion.1
  582.9 2.1 reshape.763
  585.0 156.2 %all-reduce.17.cloned.1.call-done = (bf16[1,4,32,1024]{3,2,1,0:T(8,128)(2,1)}, bf16[1,4,32,2048]{3,2,1,0:T(8,128)(2,1)}) async-done(((bf16[1,4,32,1024]{3,2,1,0:T(8,128)(2,1)}, bf16[1,4,32,2048]{3,2,1,0:T(8,128)(2,1)}), (bf16[1,4,32,1024]{3,2,1,0:T(8,128)(2,1)}, bf16[1,4,32,2048]{3,2,1,0:T(8,128)(2,1)})) %all-reduce.17.cloned.1.call-update) | async-done | bytes 786448 | tf_op jit(solution)/shard_map/psum | solution.py:206
  741.2 1.4 multiply_reduce_fusion
  743.0 1.3 broadcast_add_fusion
  744.4 2.1 reshape.764
  746.5 1.3 copy.282
  747.8 1.9 reshape.765
  749.8 1.2 add_convert_fusion
  760.3 8.2 collective-permute-start.4
  768.5 1.9 collective-permute-start.5
  770.4 1.3 convolution_bitcast_fusion.5
  772.0 1.0 copy.85
  773.2 3.3 collective-permute-done.5
  776.5 1.1 maximum_convert_fusion.1
  778.3 1.2 reshape.797
  781.4 2.2 fusion
  783.6 1.3 dynamic-slice
  785.5 1.0 dynamic-slice_reduce_fusion
  786.8 59.2 %all-gather.1 = bf16[4,32,2048]{2,1,0:T(8,128)(2,1)S(1)} all-gather(bf16[4,32,256]{2,1,0:T(8,128)(2,1)S(1)} %convolution_convert_fusion.7), channel_id=3, replica_groups=mesh['lat'=64,'tp'=8] {'tp'}, dimensions={2}, use_global_device_ids=true | all-gather | bytes 589824 | tf_op jit(solution)/shard_map/all_gather | solution.py:211
  846.0 1.0 reshape.774
  847.1 1.4 copy.283
  848.5 2.0 reshape.771
  851.5 750.8 %all-reduce.15.cloned.1.call-done = f32[512,1,192]{2,1,0:T(1,128)} async-done(((f32[512,1,192]{2,1,0:T(1,128)}), f32[512,1,192]{2,1,0:T(1,128)}) %all-reduce.15.cloned.1.call-update) | async-done | bytes 393232
  1602.3 1.3 constant_dynamic-slice_fusion
  1603.6 112.2 %reduce-scatter.7.cloned.1.call-done = bf16[8,4096]{1,0:T(8,128)(2,1)} async-done(((bf16[64,4096]{1,0:T(8,128)(2,1)}), bf16[8,4096]{1,0:T(8,128)(2,1)}) %reduce-scatter.7.cloned.1.call-update) | async-done | bytes 65552
  1716.7 1.1 multiply_reduce_fusion.6
  1717.8 1.1 fusion.184
  1718.9 1.7 add_convert_fusion.2
  1720.6 418.5 %reduce-scatter.5.cloned.1.call-done = f32[32,128]{1,0:T(8,128)} async-done(((f32[2048,128]{1,0:T(8,128)}), f32[32,128]{1,0:T(8,128)}) %reduce-scatter.5.cloned.1.call-update) | async-done | bytes 16400 | tf_op jit(solution)/shard_map/reduce_scatter | solution.py:251
  (243 shorter events, 36.6 us)
Async XLA Ops:
  7.2 349.0 %copy-start = (bf16[2048,128]{1,0:T(8,128)(2,1)S(1)}, bf16[2048,128]{1,0:T(8,128)(2,1)}, u32[]{:S(2)}) copy-start(bf16[2048,128]{1,0:T(8,128)(2,1)} %param.20) | copy-start | bytes 1572868
  7.2 172.8 %all-reduce.11.cloned.1.call-start = ((), (), s32[]{:S(2)}) async-start(), calls=%async_computation.3 | async-start | bytes 524288 | tf_op jit(solution)/shard_map/psum | solution.py:216
  8.2 2.2 copy-start.4
  11.7 11.6 copy-start.12
  12.5 13.6 collective-permute-start
  17.4 8.7 collective-permute-start.1
  23.9 1.0 copy-start.10
  26.0 323.5 %all-reduce.9.cloned.1.call-start = ((), (), s32[]{:S(2)}) async-start(), calls=%async_computation.2 | async-start | bytes 2097152 | tf_op jit(solution)/shard_map/psum | solution.py:187
  28.7 1.8 copy-start.59
  28.8 1.7 copy-start.35
  29.6 1.0 copy-start.7
  29.6 1.1 copy-start.33
  33.4 146.6 %copy-start.15 = (bf16[2,64,1024]{2,1,0:T(8,128)(2,1)S(1)}, bf16[2,64,1024]{2,1,0:T(8,128)(2,1)}, u32[]{:S(2)}) copy-start(bf16[2,64,1024]{2,1,0:T(8,128)(2,1)} %param.23) | copy-start | bytes 786436
  33.5 545.0 %all-reduce.13.cloned.1.call-start = ((), (), s32[]{:S(2)}) async-start(), calls=%async_computation.4 | async-start | bytes 524288 | tf_op jit(solution)/shard_map/psum | solution.py:242
  350.9 1.0 copy-start.2
  354.2 1.9 copy-start.1
  354.2 1.9 copy-start.30
  357.7 56.5 %copy-start.9 = (bf16[1024,2,192]{0,2,1:T(8,128)(2,1)S(1)}, bf16[1024,2,192]{0,2,1:T(8,128)(2,1)}, u32[]{:S(2)}) copy-start(bf16[1024,2,192]{0,2,1:T(8,128)(2,1)} %param.22) | copy-start | bytes 2359300
  415.0 9.9 copy-start.27
  415.1 10.6 collective-permute-start.2
  426.0 1.5 copy-start.39
  426.1 1.4 copy-start.55
  428.5 3.1 collective-permute-start.3
  432.6 1.1 copy-start.16
  432.6 308.6 %all-reduce.17.cloned.1.call-start = ((), (), s32[]{:S(2)}) async-start(), calls=%async_computation.8 | async-start | bytes 1572864 | tf_op jit(solution)/shard_map/psum | solution.py:206
  433.7 144.7 %copy-start.44 = (f32[4,32]{1,0:T(4,128)S(1)}, f32[4,32]{1,0:T(4,128)}, u32[]{:S(2)}) copy-start(f32[4,32]{1,0:T(4,128)} %copy-done.43) | copy-start | bytes 1540
  433.7 144.7 %copy-start.54 = (f32[1024]{0:T(1024)S(1)}, f32[1024]{0:T(1024)}, u32[]{:S(2)}) copy-start(f32[1024]{0:T(1024)} %param.21) | copy-start | bytes 12292
  434.7 145.0 %copy-start.52 = (f32[4,32]{1,0:T(4,128)S(1)}, f32[4,32]{1,0:T(4,128)}, u32[]{:S(2)}) copy-start(f32[4,32]{1,0:T(4,128)} %copy-done.51) | copy-start | bytes 1540
  578.4 1.3 copy-start.19
  580.7 2.0 copy-start.20
  580.7 2.0 copy-start.47
  582.7 1019.6 %all-reduce.15.cloned.1.call-start = ((), (), s32[]{:S(2)}) async-start(), calls=%async_computation.7 | async-start | bytes 1048576
  741.2 1.4 copy-start.50
  741.2 1.4 copy-start.5
  749.8 1.3 copy-start.29
  751.0 1.4 copy-start.6
  752.2 1.0 copy-start.46
  758.2 13.5 copy-start.31
  760.3 12.9 collective-permute-start.4
  768.5 8.0 collective-permute-start.5
  773.1 4.5 copy-start.23
  773.1 4.5 copy-start.32
  773.1 942.7 %reduce-scatter.7.cloned.1.call-start = ((), (), s32[]{:S(2)}) async-start(), calls=%async_computation.6 | async-start | bytes 589824
  779.5 1359.6 %reduce-scatter.5.cloned.1.call-start = ((), (), s32[]{:S(2)}) async-start(), calls=%async_computation.5 | async-start | bytes 1064960 | tf_op jit(solution)/shard_map/reduce_scatter | solution.py:251
  783.5 3.0 copy-start.11
  783.5 3.0 copy-start.26
  848.5 2.0 copy-start.3
  850.5 866.2 %copy-start.42 = (f32[512]{0:T(512)S(1)}, f32[512]{0:T(512)}, u32[]{:S(2)}) copy-start(f32[512]{0:T(512)} %param.16) | copy-start | bytes 6148
  (27 other events, 20.8 us)
Sparse Core Ops, SparseCore 0:
  26.1 153.8 all-reduce.10
  183.2 166.1 all-reduce.8
  432.7 145.6 all-reduce.12
  582.8 158.3 all-reduce.16
  773.2 828.9 all-reduce.14
  1606.6 109.1 reduce-scatter.6
  1719.4 419.6 reduce-scatter.4
where the time goes:
time: 2160 us; the launch traced here: 2150 us
  waiting for transfers between devices  1900 us (88%)
  blocking collectives  115 us (5%)
  local copies, waits for them, and re-layouts  38.3 us (2%)
  starting transfers between devices  33.3 us (2%)
  matrix products  23.1 us (1%)
    unnamed x9, waiting for transfers between devices  863 us
    reduce_scatter x1, waiting for transfers between devices, local(): lax.psum_scatter(merge_term, 'lat', scatter_dimension=0, tiled=True)  419 us
    psum x1, waiting for transfers between devices, local(): resid = hidden + lax.psum(partial_out, 'tp')  168 us
    psum x1, waiting for transfers between devices, local(): lax.psum(contract('tvxhe,hec->tvxc', coarse_heads, coarse_out).astype(jnp...  156 us
    psum x1, waiting for transfers between devices, local(): lax.psum(contract('tvxu,cu->tvxc', grad_up_own, up_weight).astype(jnp.bfl...  146 us
    psum x1, waiting for transfers between devices, local(): lax.psum(partial_cnorm.astype(jnp.bfloat16), 'tp').astype(jnp.float32)  144 us
    all_gather x1, blocking collectives, local(): upsampled = lax.all_gather(up_part, 'tp', axis=3, tiled=True)  59.2 us
    all_gather x1, blocking collectives, local(): coarse = lax.all_gather(coarse_part, 'tp', axis=3, tiled=True)  55.5 us
  transfers between devices with their start and end apart: 13, of which 10 were waited for; matrix products, arithmetic and copies ran while one was open for 2% of the time, Pallas kernels for 0%

commit v1 on v0

v1 whole, which is shorter than its diff:
```python
import functools

import jax
import jax.numpy as jnp
from jax import lax
from jax.experimental import pallas as pl
from jax.experimental.pallas import tpu as pltpu
from jax.sharding import PartitionSpec as P

MESH = pl.DeviceIdType.MESH
F32 = jnp.float32
BF16 = jnp.bfloat16
EPSILON = 1e-05
NEGATIVE = -1e30

D = 512
DC = 1024
LEV = 4
LON = 64
ZH = 2
YS = 4
TP = ZH * YS
ROW = LEV * LON
CTOK = ROW // 2
SHARE = ROW // TP
CSHARE = CTOK // TP
SCALE = 0.125


def dot(a, b):
    return lax.dot_general(a, b, (((1,), (0,)), ((), ())), preferred_element_type=F32)


def dot_nt(a, b):
    return lax.dot_general(a, b, (((1,), (1,)), ((), ())), preferred_element_type=F32)


def dot_tn(a, b):
    return lax.dot_general(a, b, (((0,), (0,)), ((), ())), preferred_element_type=F32)


def normalize(values, gain):
    centred = values - jnp.mean(values, axis=-1, keepdims=True)
    spread = jnp.mean(centred * centred, axis=-1, keepdims=True)
    return centred * lax.rsqrt(spread + EPSILON) * gain


def normalize_back(values, gain, incoming):
    centred = values - jnp.mean(values, axis=-1, keepdims=True)
    spread = jnp.mean(centred * centred, axis=-1, keepdims=True)
    inverse = lax.rsqrt(spread + EPSILON)
    unit = centred * inverse
    inner = incoming * gain
    first = jnp.mean(inner, axis=-1, keepdims=True)
    second = jnp.mean(inner * unit, axis=-1, keepdims=True)
    return inverse * (inner - first - unit * second)


class Links:
    def __init__(self, send_sems, recv_sems):
        self.send_sems, self.recv_sems = send_sems, recv_sems
        self.copies = []

    def copy(self, src, dst, device):
        at = len(self.copies)
        made = pltpu.make_async_remote_copy(
            src_ref=src,
            dst_ref=dst,
            send_sem=self.send_sems.at[at],
            recv_sem=self.recv_sems.at[at],
            device_id=device,
            device_id_type=MESH,
        )
        self.copies.append(made)
        return made

    def finish(self):
        for made in self.copies:
            made.wait_send()


class Group:
    def __init__(self, links):
        self.links = links
        self.tp = lax.axis_index("tp")
        self.zh, self.y = lax.div(self.tp, YS), lax.rem(self.tp, YS)
        self.other = lax.rem(self.tp + YS, TP)

    def y_at(self, k):
        return lax.rem(self.y + k, YS)

    def along_y(self, k):
        return {"tp": self.zh * YS + self.y_at(k)}


class Gather:
    def __init__(self, group, view):
        links = group.links
        own, far = view(group.tp), view(group.other)
        self.over_z = links.copy(own, own, {"tp": group.other})
        self.over_y = [links.copy(own, own, group.along_y(k)) for k in range(1, YS)]
        self.passed = [links.copy(far, far, group.along_y(k)) for k in range(1, YS)]

    def start(self):
        for made in [self.over_z] + self.over_y:
            made.start()

    def forward(self):
        self.over_z.wait_recv()
        for made in self.passed:
            made.start()

    def finish(self):
        for made in self.over_y + self.passed:
            made.wait_recv()


class Scatter:
    def __init__(self, group, terms, came_y, half, came_z):
        self.group, self.terms = group, terms
        self.came_y, self.half, self.came_z = came_y, half, came_z
        links = group.links
        self.over_y = [
            links.copy(terms.at[:, group.y_at(k)], came_y.at[k - 1], group.along_y(k))
            for k in range(1, YS)
        ]
        self.over_z = links.copy(half, came_z, {"tp": group.other})

    def start(self):
        for made in self.over_y:
            made.start()

    def summed(self, zh):
        total = self.terms[zh, self.group.y].astype(F32)
        for k in range(YS - 1):
            total = total + self.came_y[k, zh].astype(F32)
        return total

    def middle(self):
        for made in self.over_y:
            made.wait_recv()
        self.half[...] = self.summed(1 - self.group.zh).astype(BF16)
        self.over_z.start()

    def finish(self):
        own = self.summed(self.group.zh)
        self.over_z.wait_recv()
        return own + self.came_z[...].astype(F32)


class Exchange:
    def __init__(self, group, source, target):
        self.copies = []
        for k in range(1, TP):
            peer = lax.rem(group.tp + k, TP)
            self.copies.append(group.links.copy(source(peer), target(group.tp), {"tp": peer}))

    def start(self):
        for made in self.copies:
            made.start()

    def finish(self):
        for made in self.copies:
            made.wait_recv()


def aligned(index, size):
    return pl.ds(pl.multiple_of(index * size, size), size)


def put(ref, rows, values):
    for j in range(values.shape[1] // 128):
        ref[j, rows, :] = values[:, 128 * j : 128 * j + 128]


def get(ref, rows):
    return jnp.concatenate([ref[j, rows, :] for j in range(ref.shape[0])], axis=1)


def softmax_pair(own, other):
    largest = jnp.maximum(
        jnp.max(own, axis=-1, keepdims=True), jnp.max(other, axis=-1, keepdims=True)
    )
    own, other = jnp.exp(own - largest), jnp.exp(other - largest)
    total = jnp.sum(own, axis=-1, keepdims=True) + jnp.sum(other, axis=-1, keepdims=True)
    return own / total, other / total


def score_grads(prob_own, prob_other, grad_own, grad_other):
    mean = jnp.sum(grad_own * prob_own, axis=-1, keepdims=True)
    mean = mean + jnp.sum(grad_other * prob_other, axis=-1, keepdims=True)
    return (
        (prob_own * (grad_own - mean) * SCALE).astype(BF16),
        (prob_other * (grad_other - mean) * SCALE).astype(BF16),
    )


def low_lanes(values):
    lane = lax.broadcasted_iota(jnp.int32, values.shape, 1)
    return jnp.where(lane < 64, values, 0.0)


def high_lanes(values):
    lane = lax.broadcasted_iota(jnp.int32, values.shape, 1)
    return jnp.where(lane >= 64, values, 0.0)


def fine_mask(start):
    def window(index):
        return ((index >> 5) + 7 + ((index & 7) >> 2)) & 7

    query = lax.broadcasted_iota(jnp.int32, (CTOK, ROW), 0) + start
    key = lax.broadcasted_iota(jnp.int32, (CTOK, ROW), 1)
    return window(query) == window(key)


def main_kernel(
    lat_count,
    fields,
    classes,
    class_table,
    gain_fine,
    fine_w,
    fine_out,
    gain_merge,
    merge_weight,
    gain_coarse,
    coarse_w,
    coarse_out,
    up_weight,
    cotangent,
    next_fields,
    fields_grad,
    terms,
    send_sems,
    recv_sems,
    hid,
    cotf,
    normed,
    queries,
    keys,
    keys_sent,
    keys_came,
    prob_own,
    prob_other,
    mixture,
    heads_all,
    wexp,
    cexp,
    resid,
    merged_norm,
    coarse_all,
    coarse_f,
    lift_all,
    lift_terms,
    lift_y,
    lift_half,
    lift_z,
    ckeys,
    ckeys_came,
    cback,
    cback_came,
    cs_terms,
    cs_y,
    cs_half,
    cs_z,
    cn_terms,
    cn_y,
    cn_half,
    cn_z,
    grad_chunk,
    grad_columns,
    lifted_all,
    mn_terms,
    mn_y,
    mn_half,
    mn_z,
    up_all,
    up_wide,
    grad_mix,
    grad_mix_send,
    grad_mix_all,
    grad_mix_rows,
    grad_resid,
    grad_q,
    grad_kv,
    grad_other,
    back,
    back_came,
    gn_terms,
    gn_y,
    gn_half,
    gn_z,
):
    links = Links(send_sems, recv_sems)
    group = Group(links)
    tp = group.tp
    lat = lax.axis_index("lat")
    before, after = lax.rem(lat + lat_count - 1, lat_count), lax.rem(lat + 1, lat_count)
    twin = lat + 1 - 2 * lax.rem(lat, 2)

    barrier = pltpu.get_barrier_semaphore()
    for k in range(1, TP):
        pl.semaphore_signal(
            barrier, inc=1, device_id={"tp": lax.rem(tp + k, TP)}, device_id_type=MESH
        )
    for peer in (before, after):
        pl.semaphore_signal(barrier, inc=1, device_id={"lat": peer}, device_id_type=MESH)

    blank = jnp.zeros((TP, 64, D), BF16)
    wexp[:, 0:64] = blank
    wexp[:, 128:192] = blank
    wexp[tp, 64:128] = fine_out[...]
    for head in range(2):
        cexp[head, 0:64] = jnp.zeros((64, DC), BF16)
        cexp[head, 64:128] = coarse_out[64 * head : 64 * head + 64]

    gather_w = Gather(group, lambda at: wexp.at[at, pl.ds(64, 64)])
    lift = Scatter(group, lift_terms, lift_y, lift_half, lift_z)
    send_keys = [
        links.copy(keys_sent.at[1], keys_came.at[0], {"lat": after}),
        links.copy(keys_sent.at[0], keys_came.at[1], {"lat": before}),
    ]
    gather_heads = Gather(group, lambda at: heads_all.at[:, aligned(at, 128)])
    gather_lift = Gather(group, lambda at: lift_all.at[aligned(at, CSHARE)])
    gather_coarse = Gather(group, lambda at: coarse_all.at[:, aligned(at, 128)])
    send_ckeys = links.copy(ckeys, ckeys_came, {"lat": twin})
    send_cback = links.copy(cback, cback_came, {"lat": twin})
    csum = Scatter(group, cs_terms, cs_y, cs_half, cs_z)
    cnorm = Scatter(group, cn_terms, cn_y, cn_half, cn_z)
    columns = Exchange(
        group,
        lambda at: grad_chunk.at[:, aligned(at, 128)],
        lambda at: grad_columns.at[aligned(at, CSHARE)],
    )
    gather_lifted = Gather(group, lambda at: lifted_all.at[aligned(at, CSHARE)])
    mnorm = Scatter(group, mn_terms, mn_y, mn_half, mn_z)
    gather_up = Gather(group, lambda at: up_all.at[at])
    mix = Exchange(
        group,
        lambda at: grad_mix_send.at[:, aligned(at, 128)],
        lambda at: grad_mix_all.at[aligned(at, SHARE)],
    )
    send_back = [
        links.copy(back.at[0], back_came.at[1], {"lat": before}),
        links.copy(back.at[1], back_came.at[0], {"lat": after}),
    ]
    gnorm = Scatter(group, gn_terms, gn_y, gn_half, gn_z)

    embedded = []
    for r in range(2):
        kinds = lax.broadcasted_iota(jnp.int32, (LON, 8), 1)
        onehot = jnp.where(classes[r] == kinds, 1.0, 0.0).astype(BF16)
        embedded.append(dot(onehot, class_table[...]))
    for r in range(2):
        for level in range(LEV):
            full = fields[r, level].astype(F32) + embedded[r]
            cots = cotangent[r, level].astype(F32)
            for block in range(TP):
                at = r * ROW + block * SHARE + level * 8
                hid[at : at + 8] = full[8 * block : 8 * block + 8]
                put(cotf, pl.ds(at, 8), cots[8 * block : 8 * block + 8])

    for i in range(4):
        chunk = pl.ds(i * 128, 128)
        normed[chunk] = normalize(hid[chunk], gain_fine[...]).astype(BF16)
    for r in range(2):
        rows = pl.ds(r * ROW, ROW)
        both = dot(normed[rows], fine_w[...])
        queries[rows] = both[:, 0:128].astype(BF16)
        kv = both[:, 128:256].astype(BF16)
        keys[r] = kv
        keys_sent[r] = kv

    pl.semaphore_wait(barrier, TP + 1)
    for made in send_keys:
        made.start()
    gather_w.start()

    kind = lax.div(tp, 2)
    quad = get(cotf, pl.ds(lax.div(kind, 2) * ROW + lax.rem(kind, 2), CTOK, stride=2))
    quad = jnp.where(lax.rem(tp, 2) == 0, quad[:, 0:256], quad[:, 256:512]).astype(BF16)
    lift_terms[...] = dot_nt(quad, up_weight[...]).astype(BF16).reshape(ZH, YS, CSHARE, DC)
    lift.start()

    for made in send_keys:
        made.wait_recv()
    gather_w.forward()

    present = (lat > 0, lat < lat_count - 1)

    def attend(r, half):
        start = r * ROW + half * CTOK
        chunk = pl.ds(start, CTOK)
        mask = fine_mask(half * CTOK)
        query = queries[chunk]
        own = jnp.where(mask, dot_nt(query, keys[r]) * SCALE, NEGATIVE)
        far = dot_nt(query, keys_came[r]) * SCALE
        far = jnp.where(jnp.logical_and(mask, present[r]), far, NEGATIVE)
        own, far = softmax_pair(own, far)
        prob_own[chunk] = own
        prob_other[chunk] = far
        mixture[chunk] = dot(own.astype(BF16), keys[r]) + dot(far.astype(BF16), keys_came[r])

    for r in range(2):
        for half in range(2):
            attend(r, half)
    lane = lax.broadcasted_iota(jnp.int32, (ROW, 128), 1)
    packed = jnp.where(lane < 64, pltpu.roll(mixture[ROW : 2 * ROW], 64, 1), mixture[0:ROW])
    heads_all[:, aligned(tp, 128)] = packed.astype(BF16)
    gather_heads.start()

    lift.middle()
    gather_w.finish()
    gather_heads.forward()
    lift_chunk = lift.finish().astype(BF16)
    lift_all[aligned(tp, CSHARE)] = lift_chunk
    gather_lift.start()
    gather_heads.finish()

    for r in range(2):
        first = 64 if r == 1 else 0
        weight = wexp[:, first : first + 128].reshape(TP * 128, D)
        rows = pl.ds(r * ROW, ROW)
        put(resid, rows, hid[rows] + dot(heads_all[...], weight))

    merged = [get(resid, pl.ds(r * ROW + s, CTOK, stride=2)) for r in range(2) for s in range(2)]
    merged = jnp.concatenate(merged, axis=1)
    merged_norm[...] = normalize(merged, gain_merge[...]).astype(BF16)
    coarse_all[:, aligned(tp, 128)] = dot(merged_norm[...], merge_weight[...]).astype(BF16)
    gather_coarse.start()
    gather_lift.forward()
    gather_coarse.forward()
    gather_lift.finish()
    grad_cmix = [dot_nt(lift_all[...], cexp[head]).astype(BF16) for head in range(2)]
    gather_coarse.finish()

    coarse_f[...] = coarse_all[...].astype(F32)
    cnormed = normalize(coarse_f[...], gain_coarse[...]).astype(BF16)
    cqkv = dot(cnormed, coarse_w[...]).astype(BF16)
    cq = [cqkv[:, 256 * head : 256 * head + 128] for head in range(2)]
    for head in range(2):
        ckeys[head] = cqkv[:, 256 * head + 128 : 256 * head + 256]
    send_ckeys.start()

    row_at = lax.broadcasted_iota(jnp.int32, (CTOK, CTOK), 0)
    col_at = lax.broadcasted_iota(jnp.int32, (CTOK, CTOK), 1)
    cmask = (row_at >> 5) == (col_at >> 5)
    own_scores = [
        jnp.where(cmask, dot_nt(cq[head], ckeys[head]) * SCALE, NEGATIVE) for head in range(2)
    ]
    send_ckeys.wait_recv()
    cgrad_q, cgrad_kv = [], []
    cheads = []
    for head in range(2):
        far = jnp.where(cmask, dot_nt(cq[head], ckeys_came[head]) * SCALE, NEGATIVE)
        own, far = softmax_pair(own_scores[head], far)
        own16, far16 = own.astype(BF16), far.astype(BF16)
        grad_own = dot_nt(grad_cmix[head], ckeys[head])
        grad_far = dot_nt(grad_cmix[head], ckeys_came[head])
        ds_own, ds_far = score_grads(own, far, grad_own, grad_far)
        cback[head] = (dot_tn(ds_far, cq[head]) + dot_tn(far16, grad_cmix[head])).astype(BF16)
        cgrad_kv.append(dot_tn(ds_own, cq[head]) + dot_tn(own16, grad_cmix[head]))
        query_grad = dot(ds_own, ckeys[head]) + dot(ds_far, ckeys_came[head])
        cgrad_q.append(low_lanes(query_grad).astype(BF16))
        cheads.append((dot(own16, ckeys[head]) + dot(far16, ckeys_came[head])).astype(BF16))
    send_cback.start()
    part = dot(cheads[0], cexp[0]) + dot(cheads[1], cexp[1])
    cs_terms[...] = part.astype(BF16).reshape(ZH, YS, CSHARE, DC)
    csum.start()
    part = dot_nt(cgrad_q[0], coarse_w[:, 0:128]) + dot_nt(cgrad_q[1], coarse_w[:, 256:384])
    send_cback.wait_recv()
    for head in range(2):
        total = (cgrad_kv[head] + cback_came[head].astype(F32)).astype(BF16)
        part = part + dot_nt(total, coarse_w[:, 256 * head + 128 : 256 * head + 256])
    cn_terms[...] = part.astype(BF16).reshape(ZH, YS, CSHARE, DC)
    cnorm.start()
    csum.middle()
    cnorm.middle()

    mine = aligned(tp, CSHARE)
    coarse_chunk = coarse_f[mine]
    grad_cn = cnorm.finish()
    grad_chunk[...] = (
        lift_chunk.astype(F32) + normalize_back(coarse_chunk, gain_coarse[...], grad_cn)
    ).astype(BF16)
    columns.start()
    grad_columns[mine] = grad_chunk[:, aligned(tp, 128)]
    lifted_all[mine] = (coarse_chunk + csum.finish()).astype(BF16)
    gather_lifted.start()
    columns.finish()
    part = dot_nt(grad_columns[...], merge_weight[...])
    mn_terms[...] = part.astype(BF16).reshape(ZH, YS, CSHARE, 4 * D)
    mnorm.start()

    scale = (2 * lat_count * LEV * LON) ** -0.5
    merge_rows = 4 * D // lat_count
    weight_rows = D // lat_count
    term = dot_tn(merged_norm[...], grad_columns[...]) * scale
    terms[:, 0:merge_rows] = term.astype(BF16).reshape(lat_count, merge_rows, 128)
    gather_lifted.forward()
    mnorm.middle()
    gather_lifted.finish()
    up_all[tp] = dot(lifted_all[...], up_weight[...]).astype(BF16)
    gather_up.start()

    grad_mn = mnorm.finish()
    merged_chunk, cot_chunk = [], []
    for r in range(2):
        for s in range(2):
            some = pl.ds(r * ROW + s + tp * SHARE, CSHARE, stride=2)
            merged_chunk.append(get(resid, some))
            cot_chunk.append(get(cotf, some))
    merged_chunk = jnp.concatenate(merged_chunk, axis=1)
    cot_chunk = jnp.concatenate(cot_chunk, axis=1)
    grad_merged = normalize_back(merged_chunk, gain_merge[...], grad_mn)
    grad_quads = (cot_chunk + grad_merged).astype(BF16)
    low = wexp[:, 0:128].reshape(TP * 128, D)
    high = wexp[:, 64:192].reshape(TP * 128, D)
    for s in range(2):
        top = grad_quads[:, s * D : (s + 1) * D]
        bottom = grad_quads[:, (2 + s) * D : (3 + s) * D]
        put(grad_mix, pl.ds(s, CSHARE, stride=2), dot_nt(top, low) + dot_nt(bottom, high))
        put(grad_resid, pl.ds(s, CSHARE, stride=2), top.astype(F32))
        put(grad_resid, pl.ds(SHARE + s, CSHARE, stride=2), bottom.astype(F32))
    grad_mix_send[...] = get(grad_mix, pl.ds(0, SHARE)).astype(BF16)
    mix.start()
    grad_mix_all[aligned(tp, SHARE)] = grad_mix_send[:, aligned(tp, 128)]
    gather_up.forward()
    mix.finish()

    both = grad_mix_all[...].astype(F32)
    grad_mix_rows[0:ROW] = high_lanes(both).astype(BF16)
    grad_mix_rows[ROW : 2 * ROW] = high_lanes(pltpu.roll(both, 64, 1)).astype(BF16)

    def attend_back(r, half):
        chunk = pl.ds(r * ROW + half * CTOK, CTOK)
        query, grad_out = queries[chunk], grad_mix_rows[chunk]
        own, far = prob_own[chunk], prob_other[chunk]
        ds_own, ds_far = score_grads(
            own, far, dot_nt(grad_out, keys[r]), dot_nt(grad_out, keys_came[r])
        )
        own16, far16 = own.astype(BF16), far.astype(BF16)
        to_own = dot_tn(ds_own, query) + dot_tn(own16, grad_out)
        to_far = dot_tn(ds_far, query) + dot_tn(far16, grad_out)
        grad_q[chunk] = low_lanes(dot(ds_own, keys[r]) + dot(ds_far, keys_came[r])).astype(BF16)
        return to_own, to_far

    for r in range(2):
        own_a, far_a = attend_back(r, 0)
        own_b, far_b = attend_back(r, 1)
        back[r] = (far_a + far_b).astype(BF16)
        send_back[r].start()
        grad_other[r] = own_a + own_b
    for made in send_back:
        made.wait_recv()
    for r in range(2):
        grad_kv[pl.ds(r * ROW, ROW)] = (grad_other[r] + back_came[r].astype(F32)).astype(BF16)
    for r in range(2):
        rows = pl.ds(r * ROW, ROW)
        part = dot_nt(grad_q[rows], fine_w[:, 0:128]) + dot_nt(grad_kv[rows], fine_w[:, 128:256])
        gn_terms[:, :, r] = part.astype(BF16).reshape(ZH, YS, SHARE, D)
    gnorm.start()

    term_q = dot_tn(normed[...], grad_q[...]) * scale
    term_kv = dot_tn(normed[...], grad_kv[...]) * scale
    term = jnp.concatenate(
        [term_q.reshape(lat_count, weight_rows, 128), term_kv.reshape(lat_count, weight_rows, 128)],
        axis=1,
    )
    terms[:, merge_rows : merge_rows + 2 * weight_rows] = term.astype(BF16)
    gnorm.middle()

    gather_up.finish()
    for r in range(2):
        for s in range(2):
            for part in range(2):
                wide = up_all[4 * r + 2 * s + part].astype(F32)
                some = pl.ds(r * ROW + s, CTOK, stride=2)
                up_wide[2 * part, some, :] = wide[:, 0:128]
                up_wide[2 * part + 1, some, :] = wide[:, 128:256]
    for r in range(2):
        for level in range(LEV):
            pieces = []
            for block in range(TP):
                at = r * ROW + block * SHARE + level * 8
                pieces.append(get(resid, pl.ds(at, 8)) + get(up_wide, pl.ds(at, 8)))
            next_fields[r, level] = jnp.concatenate(pieces, axis=0).astype(BF16)

    grad_norm = gnorm.finish()
    for r in range(2):
        own_hidden = hid[pl.ds(pl.multiple_of(r * ROW + tp * SHARE, SHARE), SHARE)]
        grad_hidden = normalize_back(own_hidden, gain_fine[...], grad_norm[r])
        grad_hidden = grad_hidden + get(grad_resid, pl.ds(r * SHARE, SHARE))
        fields_grad[r] = grad_hidden.astype(BF16)
    links.finish()


def lat_kernel(
    lat_count, nx, nz, terms, out, send_sems, recv_sems, came_c, part_x, came_x, part_z, came_z
):
    links = Links(send_sems, recv_sems)
    lat = lax.axis_index("lat")
    core = lax.rem(lat, 2)
    z = lax.rem(lax.div(lat, 2), nz)
    x = lax.div(lat, 2 * nz)

    def place(x_at, z_at, core_at):
        return {"lat": (x_at * nz + z_at) * 2 + core_at}

    def x_at(k):
        return lax.rem(x + k, nx)

    def z_at(k):
        return lax.rem(z + k, nz)

    twin = place(x, z, 1 - core)
    x_peers = [place(x_at(k), z, core) for k in range(1, nx)]
    z_peers = [place(x, z_at(k), core) for k in range(1, nz)]
    barrier = pltpu.get_barrier_semaphore()
    for peer in [twin] + x_peers + z_peers:
        pl.semaphore_signal(barrier, inc=1, device_id=peer, device_id_type=MESH)
    pl.semaphore_wait(barrier, 1 + len(x_peers) + len(z_peers))

    over_core = links.copy(terms.at[:, :, 1 - core], came_c, twin)
    over_core.start()
    over_core.wait_recv()
    for i in range(nx):
        part_x[i] = (terms[i, :, core].astype(F32) + came_c[i].astype(F32)).astype(BF16)
    over_x = [
        links.copy(part_x.at[x_at(k)], came_x.at[k - 1], x_peers[k - 1]) for k in range(1, nx)
    ]
    for made in over_x:
        made.start()
    total = part_x[x].astype(F32)
    for k in range(1, nx):
        over_x[k - 1].wait_recv()
        total = total + came_x[k - 1].astype(F32)
    part_z[...] = total.astype(BF16)
    over_z = [
        links.copy(part_z.at[z_at(k)], came_z.at[k - 1], z_peers[k - 1]) for k in range(1, nz)
    ]
    for made in over_z:
        made.start()
    total = part_z[z].astype(F32)
    for k in range(1, nz):
        over_z[k - 1].wait_recv()
        total = total + came_z[k - 1].astype(F32)
    out[...] = total
    links.finish()


def vmem(*shape, kind=BF16):
    return pltpu.VMEM(shape, kind)


def scatter_buffers(*chunk):
    return [vmem(ZH, YS, *chunk), vmem(YS - 1, ZH, *chunk), vmem(*chunk), vmem(*chunk)]


def split_heads(weight):
    query, rest = weight[..., :64], weight[..., 64:]
    wide = jnp.concatenate([query, jnp.zeros_like(query), rest], axis=-1)
    return wide.reshape(weight.shape[0], -1)


def local(
    lat_count,
    fields,
    classes,
    class_table,
    gain_fine,
    fine_qkv,
    fine_out,
    gain_merge,
    merge_weight,
    gain_coarse,
    coarse_qkv,
    coarse_out,
    up_weight,
    cotangent,
):
    block_rows = 4 * D // lat_count + 2 * (D // lat_count)
    nz = min(8, lat_count // 4)
    nx = lat_count // (2 * nz)
    whole = pl.BlockSpec(memory_space=pltpu.VMEM)
    copies = 120
    scratch = [
        pltpu.SemaphoreType.DMA((copies,)),
        pltpu.SemaphoreType.DMA((copies,)),
        vmem(2 * ROW, D, kind=F32),
        vmem(4, 2 * ROW, 128, kind=F32),
        vmem(2 * ROW, D),
        vmem(2 * ROW, 128),
        vmem(2, ROW, 128),
        vmem(2, ROW, 128),
        vmem(2, ROW, 128),
        vmem(2 * ROW, ROW, kind=F32),
        vmem(2 * ROW, ROW, kind=F32),
        vmem(2 * ROW, 128, kind=F32),
        vmem(ROW, TP * 128),
        vmem(TP, 192, D),
        vmem(2, 128, DC),
        vmem(4, 2 * ROW, 128, kind=F32),
        vmem(CTOK, 4 * D),
        vmem(CTOK, DC),
        vmem(CTOK, DC, kind=F32),
        vmem(CTOK, DC),
        *scatter_buffers(CSHARE, DC),
        vmem(2, CTOK, 128),
        vmem(2, CTOK, 128),
        vmem(2, CTOK, 128),
        vmem(2, CTOK, 128),
        *scatter_buffers(CSHARE, DC),
        *scatter_buffers(CSHARE, DC),
        vmem(CSHARE, DC),
        vmem(CTOK, 128),
        vmem(CTOK, DC),
        *scatter_buffers(CSHARE, 4 * D),
        vmem(TP, CTOK, 256),
        vmem(4, 2 * ROW, 128, kind=F32),
        vmem(TP, SHARE, 128, kind=F32),
        vmem(SHARE, TP * 128),
        vmem(ROW, 128),
        vmem(2 * ROW, 128),
        vmem(4, 2 * SHARE, 128, kind=F32),
        vmem(2 * ROW, 128),
        vmem(2 * ROW, 128),
        vmem(2, ROW, 128, kind=F32),
        vmem(2, ROW, 128),
        vmem(2, ROW, 128),
        *scatter_buffers(2, SHARE, D),
    ]
    next_fields, fields_grad, terms = pl.pallas_call(
        functools.partial(main_kernel, lat_count),
        out_shape=(
            jax.ShapeDtypeStruct((2, LEV, LON, D), BF16),
            jax.ShapeDtypeStruct((2, SHARE, D), BF16),
            jax.ShapeDtypeStruct((lat_count, block_rows, 128), BF16),
        ),
        in_specs=[whole] * 13,
        out_specs=[whole] * 3,
        scratch_shapes=scratch,
        compiler_params=pltpu.CompilerParams(
            collective_id=0, has_side_effects=True, vmem_limit_bytes=56 * 2**20
        ),
    )(
        fields,
        classes.reshape(2, LON, 1),
        class_table,
        gain_fine.reshape(1, -1),
        split_heads(fine_qkv),
        fine_out.reshape(64, D),
        gain_merge.reshape(1, -1),
        merge_weight,
        gain_coarse.reshape(1, -1),
        split_heads(coarse_qkv),
        coarse_out.reshape(128, DC),
        up_weight,
        cotangent,
    )
    sums = pl.pallas_call(
        functools.partial(lat_kernel, lat_count, nx, nz),
        out_shape=jax.ShapeDtypeStruct((block_rows, 128), F32),
        in_specs=[whole],
        out_specs=whole,
        scratch_shapes=[
            pltpu.SemaphoreType.DMA((nx + nz,)),
            pltpu.SemaphoreType.DMA((nx + nz,)),
            vmem(nx, nz, block_rows, 128),
            vmem(nx, nz, block_rows, 128),
            vmem(nx - 1, nz, block_rows, 128),
            vmem(nz, block_rows, 128),
            vmem(nz - 1, block_rows, 128),
        ],
        compiler_params=pltpu.CompilerParams(collective_id=1, has_side_effects=True),
    )(terms.reshape(nx, nz, 2, block_rows, 128))
    merge_rows, weight_rows = 4 * D // lat_count, D // lat_count
    query_rows = sums[merge_rows : merge_rows + weight_rows, :64]
    weight_grad = jnp.concatenate([query_rows, sums[merge_rows + weight_rows :]], axis=-1)
    return (
        next_fields,
        fields_grad.reshape(2, LEV, LON // TP, D),
        weight_grad.reshape(weight_rows, 1, 192),
        sums[:merge_rows],
    )


def solution(mesh):
    placed = (
        P("lat", None, None, None),
        P("lat", None),
        P(),
        P(),
        P(None, "tp", None),
        P("tp", None, None),
        P(),
        P(None, "tp"),
        P(),
        P(None, "tp", None),
        P("tp", None, None),
        P(None, "tp"),
        P("lat", None, None, None),
    )
    return jax.shard_map(
        functools.partial(local, mesh.shape["lat"]),
        mesh=mesh,
        in_specs=placed,
        out_specs=(
            P("lat", None, None, None),
            P("lat", None, "tp", None),
            P("lat", "tp", None),
            P("lat", "tp"),
        ),
        check_vma=False,
    )
```

time: 2160 us -> 180 us (0.08)
  waiting for transfers between devices: 1900 us -> 0 us
  Pallas kernels: 0 us -> 168 us
  blocking collectives: 115 us -> 0 us
  starting transfers between devices: 33.3 us -> 0 us
  local copies, waits for them, and re-layouts: 38.3 us -> 9.99 us
  matrix products: 23.1 us -> 0 us
    unnamed x9 -> x0, waiting for transfers between devices: 863 us -> none
    psum x4 -> x0, waiting for transfers between devices: 614 us -> none  [the longest x1 168 us: local(): resid = hidden + lax.psum(partial_out, 'tp')]
    reduce_scatter x1 -> x0, waiting for transfers between devices: 419 us -> none  [local(): lax.psum_scatter(merge_term, 'lat', scatter_dimension=0, tiled=True)]
    pallas_call x0 -> x2, Pallas kernels: none -> 168 us  [the longest x1 141 us: local(): pl.pallas_call(functools.partial(main_kernel, lat_count), out_shape=(jax....]
    all_gather x2 -> x0, blocking collectives: 115 us -> none  [the longest x1 59.2 us: local(): upsampled = lax.all_gather(up_part, 'tp', axis=3, tiled=True)]
    ppermute x6 -> x0, starting transfers between devices: 32.9 us -> none  [the longest x2 13.1 us: extended(): before = lax.ppermute(last, axis, up)]
    dot_general x42 -> x0, matrix products: 23.1 us -> none  [the longest x41 22.1 us: contract(): jnp.einsum(pattern, operand_a, operand_b, preferred_element_type=jnp.floa...]
  transfers between devices with their start and end apart: 13 -> 0, of which waited for: 10 -> 0; matrix products, arithmetic and copies ran while one was open for 2% -> 0% of each run, Pallas kernels for 0% -> 0%
where the time goes in v1:
time: 180 us; the launch traced here: 179 us
  Pallas kernels  168 us (93%)
  local copies, waits for them, and re-layouts  9.99 us (6%)
    pallas_call x1, Pallas kernels, local(): pl.pallas_call(functools.partial(main_kernel, lat_count), out_shape=(jax....  141 us
    pallas_call x1, Pallas kernels, local(): pl.pallas_call(functools.partial(lat_kernel, lat_count, nx, nz), out_shap...  26.1 us

profile of v1, /device:TPU:1, one launch (start us, length us, event | category | flops | bytes accessed | tf_op | source)
XLA Modules:
  0.0 179.3 jit_solution(4657930947400750795)
XLA Ops:
  0.6 0.1 pad.6.clone
  0.7 1.4 copy.20.classes
  2.1 0.8 slice.21
  3.0 0.1 copy.23
  3.1 0.9 slice.22
  4.0 0.1 copy.24
  4.1 0.0 slice-start
  4.2 0.0 slice-start.1
  4.2 0.8 maximum_bitcast_fusion.fine_w
  4.9 0.2 slice-done
  5.1 0.3 slice-done.1
  5.4 0.2 pad_maximum_fusion
  5.6 1.3 copy.22.coarse_w
  6.9 141.4 %shard_map.156 = (bf16[2,4,64,512]{3,2,1,0:T(8,128)(2,1)}, bf16[2,32,512]{2,1,0:T(8,128)(2,1)}, bf16[64,48,128]{2,1,0:T(8,128)(2,1)}) custom-call(bf16[2,4,64,512]{3,2,1,0:T(8,128)(2,1)} %fields.1, s32[2,64,1]{2,1,0:T(8,128)} %copy.20.classes, bf16[8,512]{1,0:T(8,128)(2,1)} %class_table.1, f32[1,512]{1,0:T(1,128)} %bitcast.20, ...), custom_call_target="tpu_custom_call" | custom-call | tf_op jit(solution)/shard_map/pallas_call | solution.py:734
  148.4 0.0 copy-start
  148.4 0.0 copy-start.1
  148.4 26.1 %shard_map.157 = f32[48,128]{1,0:T(8,128)} custom-call(bf16[4,8,2,48,128]{4,3,2,1,0:T(8,128)(2,1)} %bitcast.14), custom_call_target="tpu_custom_call" | custom-call | tf_op jit(solution)/shard_map/pallas_call | solution.py:762
  174.5 0.7 slice.26
  175.2 0.7 slice.25
  175.9 1.3 slice.27
  177.2 0.1 maximum_bitcast_fusion.1
  177.2 0.6 copy.21
  177.9 0.0 copy-done
  177.9 0.8 copy.27
  178.7 0.0 copy-done.1
  178.7 0.6 copy.28
  (1 shorter events, 0.0 us)
Async XLA Ops:
  4.1 1.0 slice-start
  4.2 1.2 slice-start.1
  148.4 29.5 %copy-start = (bf16[2,4,64,512]{3,2,1,0:T(8,128)(2,1)S(1)}, bf16[2,4,64,512]{3,2,1,0:T(8,128)(2,1)}, u32[]{:S(2)}) copy-start(bf16[2,4,64,512]{3,2,1,0:T(8,128)(2,1)} %get-tuple-element.18) | copy-start | bytes 1572868
  148.4 30.3 %copy-start.1 = (bf16[2,32,512]{2,1,0:T(8,128)(2,1)S(1)}, bf16[2,32,512]{2,1,0:T(8,128)(2,1)}, u32[]{:S(2)}) copy-start(bf16[2,32,512]{2,1,0:T(8,128)(2,1)} %get-tuple-element.8) | copy-start | bytes 196612

commit v2 on v1

--- a/solution.py
+++ b/solution.py
@@ -164,6 +164,66 @@
             made.wait_recv()
 
 
+class LatSum:
+    def __init__(self, links, place, terms, came_x, part, came_z):
+        self.place, self.terms, self.came_x, self.part, self.came_z = (
+            place,
+            terms,
+            came_x,
+            part,
+            came_z,
+        )
+        self.over_x = [
+            links.copy(terms.at[x, :, core], came_x.at[k], place.at(x, place.z, core))
+            for k, (x, core) in enumerate(place.x_peers)
+        ]
+        self.over_z = [
+            links.copy(part.at[z], came_z.at[k], place.at(place.x, z, place.core))
+            for k, z in enumerate(place.z_peers)
+        ]
+
+    def start(self):
+        for made in self.over_x:
+            made.start()
+
+    def middle(self):
+        for made in self.over_x:
+            made.wait_recv()
+        total = self.terms[self.place.x, :, self.place.core].astype(F32)
+        for k in range(len(self.over_x)):
+            total = total + self.came_x[k].astype(F32)
+        self.part[...] = total.astype(BF16)
+        for made in self.over_z:
+            made.start()
+
+    def finish(self):
+        for made in self.over_z:
+            made.wait_recv()
+        total = self.part[self.place.z].astype(F32)
+        for k in range(len(self.over_z)):
+            total = total + self.came_z[k].astype(F32)
+        return total
+
+
+class Place:
+    def __init__(self, nx, nz):
+        lat = lax.axis_index("lat")
+        self.nz = nz
+        self.core = lax.rem(lat, 2)
+        self.z = lax.rem(lax.div(lat, 2), nz)
+        self.x = lax.div(lat, 2 * nz)
+        self.x_peers = [
+            (lax.rem(self.x + i, nx), lax.rem(self.core + j, 2))
+            for i in range(nx)
+            for j in range(2)
+            if i or j
+        ]
+        self.z_peers = [lax.rem(self.z + k, nz) for k in range(1, nz)]
+
+    def at(self, x, z, core):
+        return {"lat": (x * self.nz + z) * 2 + core}
+
+
 def aligned(index, size):
     return pl.ds(pl.multiple_of(index * size, size), size)
 
@@ -216,6 +276,8 @@
 
 def main_kernel(
     lat_count,
+    nx,
+    nz,
     fields,
     classes,
     class_table,
@@ -231,7 +293,8 @@
     cotangent,
     next_fields,
     fields_grad,
-    terms,
+    fine_grad,
+    merge_grad,
     send_sems,
     recv_sems,
     hid,
@@ -291,6 +354,14 @@
     gn_y,
     gn_half,
     gn_z,
+    mterms,
+    mcame_x,
+    mpart,
+    mcame_z,
+    fterms,
+    fcame_x,
+    fpart,
+    fcame_z,
 ):
     links = Links(send_sems, recv_sems)
     group = Group(links)
@@ -304,8 +375,12 @@
         pl.semaphore_signal(
             barrier, inc=1, device_id={"tp": lax.rem(tp + k, TP)}, device_id_type=MESH
         )
-    for peer in (before, after):
-        pl.semaphore_signal(barrier, inc=1, device_id={"lat": peer}, device_id_type=MESH)
+    place = Place(nx, nz)
+    lat_peers = [{"lat": before}, {"lat": after}]
+    lat_peers += [place.at(x, place.z, core) for x, core in place.x_peers]
+    lat_peers += [place.at(place.x, z, place.core) for z in place.z_peers]
+    for peer in lat_peers:
+        pl.semaphore_signal(barrier, inc=1, device_id=peer, device_id_type=MESH)
 
     blank = jnp.zeros((TP, 64, D), BF16)
     wexp[:, 0:64] = blank
@@ -346,12 +421,14 @@
         links.copy(back.at[1], back_came.at[0], {"lat": after}),
     ]
     gnorm = Scatter(group, gn_terms, gn_y, gn_half, gn_z)
+    merge_sum = LatSum(links, place, mterms, mcame_x, mpart, mcame_z)
+    fine_sum = LatSum(links, place, fterms, fcame_x, fpart, fcame_z)
 
     embedded = []
     for r in range(2):
-        kinds = lax.broadcasted_iota(jnp.int32, (LON, 8), 1)
-        onehot = jnp.where(classes[r] == kinds, 1.0, 0.0).astype(BF16)
-        embedded.append(dot(onehot, class_table[...]))
+        kinds = lax.broadcasted_iota(jnp.int32, (8, LON), 0)
+        onehot = jnp.where(classes[r : r + 1, :] == kinds, 1.0, 0.0).astype(BF16)
+        embedded.append(dot_tn(onehot, class_table[...]))
     for r in range(2):
         for level in range(LEV):
             full = fields[r, level].astype(F32) + embedded[r]
@@ -366,13 +443,12 @@
         normed[chunk] = normalize(hid[chunk], gain_fine[...]).astype(BF16)
     for r in range(2):
         rows = pl.ds(r * ROW, ROW)
-        both = dot(normed[rows], fine_w[...])
-        queries[rows] = both[:, 0:128].astype(BF16)
-        kv = both[:, 128:256].astype(BF16)
+        queries[rows] = low_lanes(dot_nt(normed[rows], fine_w[0:128])).astype(BF16)
+        kv = dot_nt(normed[rows], fine_w[64:192]).astype(BF16)
         keys[r] = kv
         keys_sent[r] = kv
 
-    pl.semaphore_wait(barrier, TP + 1)
+    pl.semaphore_wait(barrier, TP - 1 + len(lat_peers))
     for made in send_keys:
         made.start()
     gather_w.start()
@@ -437,11 +513,10 @@
 
     coarse_f[...] = coarse_all[...].astype(F32)
     cnormed = normalize(coarse_f[...], gain_coarse[...]).astype(BF16)
-    cqkv = dot(cnormed, coarse_w[...]).astype(BF16)
-    cq = [cqkv[:, 256 * head : 256 * head + 128] for head in range(2)]
     for head in range(2):
-        ckeys[head] = cqkv[:, 256 * head + 128 : 256 * head + 256]
+        ckeys[head] = dot_nt(cnormed, coarse_w[head, 64:192]).astype(BF16)
     send_ckeys.start()
+    cq = [low_lanes(dot_nt(cnormed, coarse_w[head, 0:128])).astype(BF16) for head in range(2)]
 
     row_at = lax.broadcasted_iota(jnp.int32, (CTOK, CTOK), 0)
     col_at = lax.broadcasted_iota(jnp.int32, (CTOK, CTOK), 1)
@@ -468,11 +543,11 @@
     part = dot(cheads[0], cexp[0]) + dot(cheads[1], cexp[1])
     cs_terms[...] = part.astype(BF16).reshape(ZH, YS, CSHARE, DC)
     csum.start()
-    part = dot_nt(cgrad_q[0], coarse_w[:, 0:128]) + dot_nt(cgrad_q[1], coarse_w[:, 256:384])
+    part = dot(cgrad_q[0], coarse_w[0, 0:128]) + dot(cgrad_q[1], coarse_w[1, 0:128])
     send_cback.wait_recv()
     for head in range(2):
         total = (cgrad_kv[head] + cback_came[head].astype(F32)).astype(BF16)
-        part = part + dot_nt(total, coarse_w[:, 256 * head + 128 : 256 * head + 256])
+        part = part + dot(total, coarse_w[head, 64:192])
     cn_terms[...] = part.astype(BF16).reshape(ZH, YS, CSHARE, DC)
     cnorm.start()
     csum.middle()
@@ -497,7 +572,8 @@
     merge_rows = 4 * D // lat_count
     weight_rows = D // lat_count
     term = dot_tn(merged_norm[...], grad_columns[...]) * scale
-    terms[:, 0:merge_rows] = term.astype(BF16).reshape(lat_count, merge_rows, 128)
+    mterms[...] = term.astype(BF16).reshape(nx, nz, 2, merge_rows, 128)
+    merge_sum.start()
     gather_lifted.forward()
     mnorm.middle()
     gather_lifted.finish()
@@ -527,6 +603,7 @@
     mix.start()
     grad_mix_all[aligned(tp, SHARE)] = grad_mix_send[:, aligned(tp, 128)]
     gather_up.forward()
+    merge_sum.middle()
     mix.finish()
 
     both = grad_mix_all[...].astype(F32)
@@ -558,7 +635,7 @@
         grad_kv[pl.ds(r * ROW, ROW)] = (grad_other[r] + back_came[r].astype(F32)).astype(BF16)
     for r in range(2):
         rows = pl.ds(r * ROW, ROW)
-        part = dot_nt(grad_q[rows], fine_w[:, 0:128]) + dot_nt(grad_kv[rows], fine_w[:, 128:256])
+        part = dot(grad_q[rows], fine_w[0:128]) + dot(grad_kv[rows], fine_w[64:192])
         gn_terms[:, :, r] = part.astype(BF16).reshape(ZH, YS, SHARE, D)
     gnorm.start()
 
@@ -568,8 +645,10 @@
         [term_q.reshape(lat_count, weight_rows, 128), term_kv.reshape(lat_count, weight_rows, 128)],
         axis=1,
     )
-    terms[:, merge_rows : merge_rows + 2 * weight_rows] = term.astype(BF16)
+    fterms[...] = term.astype(BF16).reshape(nx, nz, 2, 2 * weight_rows, 128)
+    fine_sum.start()
     gnorm.middle()
+    fine_sum.middle()
 
     gather_up.finish()
     for r in range(2):
@@ -593,60 +672,10 @@
         grad_hidden = normalize_back(own_hidden, gain_fine[...], grad_norm[r])
         grad_hidden = grad_hidden + get(grad_resid, pl.ds(r * SHARE, SHARE))
         fields_grad[r] = grad_hidden.astype(BF16)
-    links.finish()
-
-
-def lat_kernel(
-    lat_count, nx, nz, terms, out, send_sems, recv_sems, came_c, part_x, came_x, part_z, came_z
-):
-    links = Links(send_sems, recv_sems)
-    lat = lax.axis_index("lat")
-    core = lax.rem(lat, 2)
-    z = lax.rem(lax.div(lat, 2), nz)
-    x = lax.div(lat, 2 * nz)
-
-    def place(x_at, z_at, core_at):
-        return {"lat": (x_at * nz + z_at) * 2 + core_at}
-
-    def x_at(k):
-        return lax.rem(x + k, nx)
-
-    def z_at(k):
-        return lax.rem(z + k, nz)
-
-    twin = place(x, z, 1 - core)
-    x_peers = [place(x_at(k), z, core) for k in range(1, nx)]
-    z_peers = [place(x, z_at(k), core) for k in range(1, nz)]
-    barrier = pltpu.get_barrier_semaphore()
-    for peer in [twin] + x_peers + z_peers:
-        pl.semaphore_signal(barrier, inc=1, device_id=peer, device_id_type=MESH)
-    pl.semaphore_wait(barrier, 1 + len(x_peers) + len(z_peers))
-
-    over_core = links.copy(terms.at[:, :, 1 - core], came_c, twin)
-    over_core.start()
-    over_core.wait_recv()
-    for i in range(nx):
-        part_x[i] = (terms[i, :, core].astype(F32) + came_c[i].astype(F32)).astype(BF16)
-    over_x = [
-        links.copy(part_x.at[x_at(k)], came_x.at[k - 1], x_peers[k - 1]) for k in range(1, nx)
-    ]
-    for made in over_x:
-        made.start()
-    total = part_x[x].astype(F32)
-    for k in range(1, nx):
-        over_x[k - 1].wait_recv()
-        total = total + came_x[k - 1].astype(F32)
-    part_z[...] = total.astype(BF16)
-    over_z = [
-        links.copy(part_z.at[z_at(k)], came_z.at[k - 1], z_peers[k - 1]) for k in range(1, nz)
-    ]
-    for made in over_z:
-        made.start()
-    total = part_z[z].astype(F32)
-    for k in range(1, nz):
-        over_z[k - 1].wait_recv()
-        total = total + came_z[k - 1].astype(F32)
-    out[...] = total
+    merge_grad[...] = merge_sum.finish()
+    sums = fine_sum.finish()
+    fine_grad[:, 0, 0:64] = sums[0:weight_rows, 0:64]
+    fine_grad[:, 0, 64:192] = sums[weight_rows : 2 * weight_rows]
     links.finish()
 
 
@@ -658,10 +687,13 @@
     return [vmem(ZH, YS, *chunk), vmem(YS - 1, ZH, *chunk), vmem(*chunk), vmem(*chunk)]
 
 
-def split_heads(weight):
-    query, rest = weight[..., :64], weight[..., 64:]
-    wide = jnp.concatenate([query, jnp.zeros_like(query), rest], axis=-1)
-    return wide.reshape(weight.shape[0], -1)
+def lat_buffers(nx, nz, rows):
+    return [
+        vmem(nx, nz, 2, rows, 128),
+        vmem(2 * nx - 1, nz, rows, 128),
+        vmem(nz, rows, 128),
+        vmem(nz - 1, rows, 128),
+    ]
 
 
 def local(
@@ -680,11 +712,11 @@
     up_weight,
     cotangent,
 ):
-    block_rows = 4 * D // lat_count + 2 * (D // lat_count)
+    merge_rows, weight_rows = 4 * D // lat_count, D // lat_count
     nz = min(8, lat_count // 4)
     nx = lat_count // (2 * nz)
     whole = pl.BlockSpec(memory_space=pltpu.VMEM)
-    copies = 120
+    copies = 160
     scratch = [
         pltpu.SemaphoreType.DMA((copies,)),
         pltpu.SemaphoreType.DMA((copies,)),
@@ -730,60 +762,40 @@
         vmem(2, ROW, 128),
         vmem(2, ROW, 128),
         *scatter_buffers(2, SHARE, D),
+        *lat_buffers(nx, nz, merge_rows),
+        *lat_buffers(nx, nz, 2 * weight_rows),
     ]
-    next_fields, fields_grad, terms = pl.pallas_call(
-        functools.partial(main_kernel, lat_count),
+    next_fields, fields_grad, fine_grad, merge_grad = pl.pallas_call(
+        functools.partial(main_kernel, lat_count, nx, nz),
         out_shape=(
             jax.ShapeDtypeStruct((2, LEV, LON, D), BF16),
             jax.ShapeDtypeStruct((2, SHARE, D), BF16),
-            jax.ShapeDtypeStruct((lat_count, block_rows, 128), BF16),
+            jax.ShapeDtypeStruct((weight_rows, 1, 192), F32),
+            jax.ShapeDtypeStruct((merge_rows, 128), F32),
         ),
         in_specs=[whole] * 13,
-        out_specs=[whole] * 3,
+        out_specs=[whole] * 4,
         scratch_shapes=scratch,
+        name="block",
         compiler_params=pltpu.CompilerParams(
             collective_id=0, has_side_effects=True, vmem_limit_bytes=56 * 2**20
         ),
     )(
         fields,
-        classes.reshape(2, LON, 1),
+        classes,
         class_table,
         gain_fine.reshape(1, -1),
-        split_heads(fine_qkv),
+        fine_qkv.reshape(D, 192).T,
         fine_out.reshape(64, D),
         gain_merge.reshape(1, -1),
         merge_weight,
         gain_coarse.reshape(1, -1),
-        split_heads(coarse_qkv),
+        coarse_qkv.transpose(1, 2, 0),
         coarse_out.reshape(128, DC),
         up_weight,
         cotangent,
     )
-    sums = pl.pallas_call(
-        functools.partial(lat_kernel, lat_count, nx, nz),
-        out_shape=jax.ShapeDtypeStruct((block_rows, 128), F32),
-        in_specs=[whole],
-        out_specs=whole,
-        scratch_shapes=[
-            pltpu.SemaphoreType.DMA((nx + nz,)),
-            pltpu.SemaphoreType.DMA((nx + nz,)),
-            vmem(nx, nz, block_rows, 128),
-            vmem(nx, nz, block_rows, 128),
-            vmem(nx - 1, nz, block_rows, 128),
-            vmem(nz, block_rows, 128),
-            vmem(nz - 1, block_rows, 128),
-        ],
-        compiler_params=pltpu.CompilerParams(collective_id=1, has_side_effects=True),
-    )(terms.reshape(nx, nz, 2, block_rows, 128))
-    merge_rows, weight_rows = 4 * D // lat_count, D // lat_count
-    query_rows = sums[merge_rows : merge_rows + weight_rows, :64]
-    weight_grad = jnp.concatenate([query_rows, sums[merge_rows + weight_rows :]], axis=-1)
-    return (
-        next_fields,
-        fields_grad.reshape(2, LEV, LON // TP, D),
-        weight_grad.reshape(weight_rows, 1, 192),
-        sums[:merge_rows],
-    )
+    return next_fields, fields_grad.reshape(2, LEV, LON // TP, D), fine_grad, merge_grad
 
 
 def solution(mesh):

time: 180 us -> 151 us (0.84); the launches traced: 179 us -> 148 us
  Pallas kernels: 168 us -> 144 us
  local copies, waits for them, and re-layouts: 9.99 us -> 3.93 us
    pallas_call x2 -> x1, Pallas kernels: 168 us -> 144 us  [local(): pl.pallas_call(functools.partial(main_kernel, lat_count, nx, nz), out_sha...]
    slice x9 -> x0, local copies, waits for them, and re-layouts: 4.89 us -> none  [the longest x6 2.21 us: split_heads(): query, rest = (weight[..., :64], weight[..., 64:])]
    reshape x2 -> x0, local copies, waits for them, and re-layouts: 2.74 us -> none  [the longest x1 1.41 us: local(): classes.reshape(2, LON, 1)]
    unnamed x9 -> x10, local copies, waits for them, and re-layouts: 2.28 us -> 3.93 us
where the time goes in v2:
time: 151 us; the launch traced here: 148 us
  Pallas kernels  144 us (95%)
  local copies, waits for them, and re-layouts  3.93 us (3%)
    pallas_call x1, Pallas kernels, local(): pl.pallas_call(functools.partial(main_kernel, lat_count, nx, nz), out_sha...  144 us
    unnamed x10, local copies, waits for them, and re-layouts  3.93 us

profile of v2, /device:TPU:1, one launch (start us, length us, event | category | flops | bytes accessed | tf_op | source)
XLA Modules:
  0.0 148.4 jit_solution(5411833822236838688)
XLA Ops:
  0.6 143.8 %block.1 = (bf16[2,4,64,512]{3,2,1,0:T(8,128)(2,1)}, bf16[2,32,512]{2,1,0:T(8,128)(2,1)}, f32[8,1,192]{2,1,0:T(1,128)}, f32[32,128]{1,0:T(8,128)}) custom-call(bf16[2,4,64,512]{3,2,1,0:T(8,128)(2,1)} %fields.1, s32[2,64]{1,0:T(2,128)} %classes.1, bf16[8,512]{1,0:T(8,128)(2,1)} %class_table.1, f32[1,512]{1,0:T(1,128)} %bitcast.17, bf16[192,512]{1,0:T(8,128)(2,1)} %bitcast.12, ...), custom_call_target="tpu_custom_call" | custom-call | tf_op jit(solution)/shard_map/block/pallas_call | solution.py:768
  144.5 0.0 copy-start
  144.5 1.9 %copy.21 = bf16[2,4,64,512]{3,2,1,0:T(8,128)(2,1)} copy(bf16[2,4,64,512]{3,2,1,0:T(8,128)(2,1)} %get-tuple-element.16) | data formatting | bytes 1048576
  146.4 0.0 copy-done
  146.4 0.0 copy-start.2
  146.4 0.6 copy.22
  147.0 0.1 copy-done.2
  147.1 0.0 copy-start.1
  147.1 0.6 copy.23
  147.7 0.1 copy-done.1
  147.8 0.6 copy.24
Async XLA Ops:
  144.5 1.9 %copy-start = (bf16[2,32,512]{2,1,0:T(8,128)(2,1)S(1)}, bf16[2,32,512]{2,1,0:T(8,128)(2,1)}, u32[]{:S(2)}) copy-start(bf16[2,32,512]{2,1,0:T(8,128)(2,1)} %get-tuple-element.9) | copy-start | bytes 196612
  146.4 0.7 copy-start.2
  147.1 0.7 copy-start.1

commit v3 on v2

--- a/solution.py
+++ b/solution.py
@@ -39,17 +39,15 @@
     return lax.dot_general(a, b, (((0,), (0,)), ((), ())), preferred_element_type=F32)
 
 
-def normalize(values, gain):
-    centred = values - jnp.mean(values, axis=-1, keepdims=True)
-    spread = jnp.mean(centred * centred, axis=-1, keepdims=True)
-    return centred * lax.rsqrt(spread + EPSILON) * gain
-
-
-def normalize_back(values, gain, incoming):
+def standardize(values):
     centred = values - jnp.mean(values, axis=-1, keepdims=True)
     spread = jnp.mean(centred * centred, axis=-1, keepdims=True)
     inverse = lax.rsqrt(spread + EPSILON)
-    unit = centred * inverse
+    return centred * inverse, inverse
+
+
+def normalize_back(values, gain, incoming):
+    unit, inverse = standardize(values)
     inner = incoming * gain
     first = jnp.mean(inner, axis=-1, keepdims=True)
     second = jnp.mean(inner * unit, axis=-1, keepdims=True)
@@ -148,20 +146,38 @@
         return own + self.came_z[...].astype(F32)
 
 
-class Exchange:
-    def __init__(self, group, source, target):
-        self.copies = []
-        for k in range(1, TP):
-            peer = lax.rem(group.tp + k, TP)
-            self.copies.append(group.links.copy(source(peer), target(group.tp), {"tp": peer}))
-
-    def start(self):
-        for made in self.copies:
+class Moments:
+    def __init__(self, group, own, came_y, half, came_z):
+        self.own, self.came_y, self.half, self.came_z = own, came_y, half, came_z
+        links = group.links
+        self.over_y = [
+            links.copy(own, came_y.at[k - 1], group.along_y(k)) for k in range(1, YS)
+        ]
+        self.over_z = links.copy(half, came_z, {"tp": group.other})
+
+    def start(self, inner, unit):
+        first = jnp.mean(inner, axis=-1, keepdims=True)
+        second = jnp.mean(inner * unit, axis=-1, keepdims=True)
+        lane = lax.broadcasted_iota(jnp.int32, (CTOK, 128), 1)
+        both = jnp.where(lane == 0, first, jnp.where(lane == 1, second, 0.0))
+        self.own[...] = both.T[0:8]
+        for made in self.over_y:
             made.start()
 
+    def middle(self):
+        for made in self.over_y:
+            made.wait_recv()
+        total = self.own[...]
+        for k in range(YS - 1):
+            total = total + self.came_y[k]
+        self.half[...] = total
+        self.over_z.start()
+
     def finish(self):
-        for made in self.copies:
-            made.wait_recv()
+        self.over_z.wait_recv()
+        total = self.half[...] + self.came_z[...]
+        both = jnp.concatenate([total, jnp.zeros((CTOK - 8, 128), F32)], axis=0).T
+        return both[:, 0:1], both[:, 1:2]
 
 
 class LatSum:
@@ -285,18 +301,24 @@
     fine_w,
     fine_out,
     gain_merge,
-    merge_weight,
+    merge_weight_in,
     gain_coarse,
-    coarse_w,
-    coarse_out,
-    up_weight,
-    cotangent,
+    coarse_w_in,
+    coarse_out_in,
+    up_weight_in,
+    cotangent_in,
     next_fields,
     fields_grad,
     fine_grad,
     merge_grad,
     send_sems,
     recv_sems,
+    local_sems,
+    merge_weight,
+    coarse_w,
+    up_weight,
+    cotangent,
+    fields_out,
     hid,
     cotf,
     normed,
@@ -331,7 +353,12 @@
     cn_y,
     cn_half,
     cn_z,
-    grad_chunk,
+    cunit,
+    cinverse,
+    cm_own,
+    cm_y,
+    cm_half,
+    cm_z,
     grad_columns,
     lifted_all,
     mn_terms,
@@ -340,9 +367,17 @@
     mn_z,
     up_all,
     up_wide,
+    munit,
+    minverse,
+    mm_own,
+    mm_y,
+    mm_half,
+    mm_z,
+    gh_terms,
+    gh_y,
+    gh_half,
+    gh_z,
     grad_mix,
-    grad_mix_send,
-    grad_mix_all,
     grad_mix_rows,
     grad_resid,
     grad_q,
@@ -363,6 +398,19 @@
     fpart,
     fcame_z,
 ):
+    def fetch(src, dst, at):
+        made = pltpu.make_async_copy(src, dst, local_sems.at[at])
+        made.start()
+        return made
+
+    got_cotangent = fetch(cotangent_in, cotangent, 0)
+    got_up = fetch(up_weight_in, up_weight, 1)
+    got_merge = fetch(merge_weight_in, merge_weight, 2)
+    got_coarse = [fetch(coarse_w_in, coarse_w, 3)]
+    for head in range(2):
+        rows = coarse_out_in.at[pl.ds(64 * head, 64)]
+        got_coarse.append(fetch(rows, cexp.at[head, pl.ds(64, 64)], 4 + head))
+
     links = Links(send_sems, recv_sems)
     group = Group(links)
     tp = group.tp
@@ -388,7 +436,6 @@
     wexp[tp, 64:128] = fine_out[...]
     for head in range(2):
         cexp[head, 0:64] = jnp.zeros((64, DC), BF16)
-        cexp[head, 64:128] = coarse_out[64 * head : 64 * head + 64]
 
     gather_w = Gather(group, lambda at: wexp.at[at, pl.ds(64, 64)])
     lift = Scatter(group, lift_terms, lift_y, lift_half, lift_z)
@@ -396,31 +443,31 @@
         links.copy(keys_sent.at[1], keys_came.at[0], {"lat": after}),
         links.copy(keys_sent.at[0], keys_came.at[1], {"lat": before}),
     ]
-    gather_heads = Gather(group, lambda at: heads_all.at[:, aligned(at, 128)])
+    gather_heads = [
+        Gather(group, lambda at, i=i: heads_all.at[pl.ds(i * 128, 128), aligned(at, 128)])
+        for i in range(2)
+    ]
     gather_lift = Gather(group, lambda at: lift_all.at[aligned(at, CSHARE)])
     gather_coarse = Gather(group, lambda at: coarse_all.at[:, aligned(at, 128)])
     send_ckeys = links.copy(ckeys, ckeys_came, {"lat": twin})
     send_cback = links.copy(cback, cback_came, {"lat": twin})
     csum = Scatter(group, cs_terms, cs_y, cs_half, cs_z)
     cnorm = Scatter(group, cn_terms, cn_y, cn_half, cn_z)
-    columns = Exchange(
-        group,
-        lambda at: grad_chunk.at[:, aligned(at, 128)],
-        lambda at: grad_columns.at[aligned(at, CSHARE)],
-    )
+    cmoments = Moments(group, cm_own, cm_y, cm_half, cm_z)
     gather_lifted = Gather(group, lambda at: lifted_all.at[aligned(at, CSHARE)])
     mnorm = Scatter(group, mn_terms, mn_y, mn_half, mn_z)
     gather_up = Gather(group, lambda at: up_all.at[at])
-    mix = Exchange(
-        group,
-        lambda at: grad_mix_send.at[:, aligned(at, 128)],
-        lambda at: grad_mix_all.at[aligned(at, SHARE)],
-    )
+    mmoments = Moments(group, mm_own, mm_y, mm_half, mm_z)
+    gheads = [
+        Scatter(group, gh_terms.at[s], gh_y.at[s], gh_half.at[s], gh_z.at[s]) for s in range(2)
+    ]
     send_back = [
         links.copy(back.at[0], back_came.at[1], {"lat": before}),
         links.copy(back.at[1], back_came.at[0], {"lat": after}),
     ]
-    gnorm = Scatter(group, gn_terms, gn_y, gn_half, gn_z)
+    gnorm = [
+        Scatter(group, gn_terms.at[r], gn_y.at[r], gn_half.at[r], gn_z.at[r]) for r in range(2)
+    ]
     merge_sum = LatSum(links, place, mterms, mcame_x, mpart, mcame_z)
     fine_sum = LatSum(links, place, fterms, fcame_x, fpart, fcame_z)
 
@@ -432,15 +479,14 @@
     for r in range(2):
         for level in range(LEV):
             full = fields[r, level].astype(F32) + embedded[r]
-            cots = cotangent[r, level].astype(F32)
             for block in range(TP):
                 at = r * ROW + block * SHARE + level * 8
                 hid[at : at + 8] = full[8 * block : 8 * block + 8]
-                put(cotf, pl.ds(at, 8), cots[8 * block : 8 * block + 8])
 
     for i in range(4):
         chunk = pl.ds(i * 128, 128)
-        normed[chunk] = normalize(hid[chunk], gain_fine[...]).astype(BF16)
+        unit, _ = standardize(hid[chunk])
+        normed[chunk] = (unit * gain_fine[...]).astype(BF16)
     for r in range(2):
         rows = pl.ds(r * ROW, ROW)
         queries[rows] = low_lanes(dot_nt(normed[rows], fine_w[0:128])).astype(BF16)
@@ -453,6 +499,14 @@
         made.start()
     gather_w.start()
 
+    got_cotangent.wait()
+    got_up.wait()
+    for r in range(2):
+        for level in range(LEV):
+            cots = cotangent[r, level].astype(F32)
+            for block in range(TP):
+                at = r * ROW + block * SHARE + level * 8
+                put(cotf, pl.ds(at, 8), cots[8 * block : 8 * block + 8])
     kind = lax.div(tp, 2)
     quad = get(cotf, pl.ds(lax.div(kind, 2) * ROW + lax.rem(kind, 2), CTOK, stride=2))
     quad = jnp.where(lax.rem(tp, 2) == 0, quad[:, 0:256], quad[:, 256:512]).astype(BF16)
@@ -484,15 +538,21 @@
     lane = lax.broadcasted_iota(jnp.int32, (ROW, 128), 1)
     packed = jnp.where(lane < 64, pltpu.roll(mixture[ROW : 2 * ROW], 64, 1), mixture[0:ROW])
     heads_all[:, aligned(tp, 128)] = packed.astype(BF16)
-    gather_heads.start()
+    for part in gather_heads:
+        part.over_z.start()
+    for part in gather_heads:
+        for made in part.over_y:
+            made.start()
 
     lift.middle()
     gather_w.finish()
-    gather_heads.forward()
+    for part in gather_heads:
+        part.forward()
     lift_chunk = lift.finish().astype(BF16)
     lift_all[aligned(tp, CSHARE)] = lift_chunk
     gather_lift.start()
-    gather_heads.finish()
+    for part in gather_heads:
+        part.finish()
 
     for r in range(2):
         first = 64 if r == 1 else 0
@@ -502,20 +562,29 @@
 
     merged = [get(resid, pl.ds(r * ROW + s, CTOK, stride=2)) for r in range(2) for s in range(2)]
     merged = jnp.concatenate(merged, axis=1)
-    merged_norm[...] = normalize(merged, gain_merge[...]).astype(BF16)
+    unit, inverse = standardize(merged)
+    merged_norm[...] = (unit * gain_merge[...]).astype(BF16)
+    got_merge.wait()
     coarse_all[:, aligned(tp, 128)] = dot(merged_norm[...], merge_weight[...]).astype(BF16)
     gather_coarse.start()
+    munit[...] = unit
+    minverse[...] = jnp.broadcast_to(inverse, (CTOK, 128))
     gather_lift.forward()
     gather_coarse.forward()
     gather_lift.finish()
+    for made in got_coarse:
+        made.wait()
     grad_cmix = [dot_nt(lift_all[...], cexp[head]).astype(BF16) for head in range(2)]
     gather_coarse.finish()
 
     coarse_f[...] = coarse_all[...].astype(F32)
-    cnormed = normalize(coarse_f[...], gain_coarse[...]).astype(BF16)
+    unit, inverse = standardize(coarse_f[...])
+    cnormed = (unit * gain_coarse[...]).astype(BF16)
     for head in range(2):
         ckeys[head] = dot_nt(cnormed, coarse_w[head, 64:192]).astype(BF16)
     send_ckeys.start()
+    cunit[...] = unit
+    cinverse[...] = jnp.broadcast_to(inverse, (CTOK, 128))
     cq = [low_lanes(dot_nt(cnormed, coarse_w[head, 0:128])).astype(BF16) for head in range(2)]
 
     row_at = lax.broadcasted_iota(jnp.int32, (CTOK, CTOK), 0)
@@ -548,25 +617,57 @@
     for head in range(2):
         total = (cgrad_kv[head] + cback_came[head].astype(F32)).astype(BF16)
         part = part + dot(total, coarse_w[head, 64:192])
-    cn_terms[...] = part.astype(BF16).reshape(ZH, YS, CSHARE, DC)
+    for t in range(TP):
+        cn_terms[t // YS, t % YS] = part[:, 128 * t : 128 * t + 128].astype(BF16)
     cnorm.start()
+    cmoments.start(part * gain_coarse[...], cunit[...])
+
+    own_low, own_high = wexp[tp, 0:128], wexp[tp, 64:192]
+
+    def own_head(top, bottom):
+        return dot_nt(top.astype(BF16), own_low) + dot_nt(bottom.astype(BF16), own_high)
+
+    head_cot, head_unit = [], []
+    for s in range(2):
+        top, bottom = [get(cotf, pl.ds(r * ROW + s, CTOK, stride=2)) for r in range(2)]
+        head_cot.append(own_head(top, bottom))
+        top, bottom = [munit[:, (2 * r + s) * D : (2 * r + s + 1) * D] for r in range(2)]
+        head_unit.append(own_head(top, bottom))
+    ones = jnp.ones((8, D), BF16)
+    head_ones = own_head(ones, ones)[0:1]
+
+    cnorm.middle()
+    cmoments.middle()
     csum.middle()
-    cnorm.middle()
-
-    mine = aligned(tp, CSHARE)
-    coarse_chunk = coarse_f[mine]
-    grad_cn = cnorm.finish()
-    grad_chunk[...] = (
-        lift_chunk.astype(F32) + normalize_back(coarse_chunk, gain_coarse[...], grad_cn)
-    ).astype(BF16)
-    columns.start()
-    grad_columns[mine] = grad_chunk[:, aligned(tp, 128)]
-    lifted_all[mine] = (coarse_chunk + csum.finish()).astype(BF16)
-    gather_lifted.start()
-    columns.finish()
+
+    lane_block = aligned(tp, 128)
+    inner = cnorm.finish() * gain_coarse[:, lane_block]
+    first, second = cmoments.finish()
+    inner = cinverse[...] * (inner - first - cunit[:, lane_block] * second)
+    grad_columns[...] = (lift_all[:, lane_block].astype(F32) + inner).astype(BF16)
+
     part = dot_nt(grad_columns[...], merge_weight[...])
+    inner = part * gain_merge[...]
+    inner16 = inner.astype(BF16)
+    low = wexp[:, 0:128].reshape(TP * 128, D)
+    high = wexp[:, 64:192].reshape(TP * 128, D)
+    for s in range(2):
+        top, bottom = [inner16[:, (2 * r + s) * D : (2 * r + s + 1) * D] for r in range(2)]
+        heads = (dot_nt(top, low) + dot_nt(bottom, high)).astype(BF16)
+        for t in range(TP):
+            gh_terms[s, t // YS, t % YS] = heads[:, 128 * t : 128 * t + 128]
+        gheads[s].start()
+    mmoments.start(inner, munit[...])
     mn_terms[...] = part.astype(BF16).reshape(ZH, YS, CSHARE, 4 * D)
     mnorm.start()
+
+    mine = aligned(tp, CSHARE)
+    lifted_all[mine] = (coarse_f[mine] + csum.finish()).astype(BF16)
+    for part in gheads:
+        part.middle()
+    mmoments.middle()
+    gather_lifted.start()
+    mnorm.middle()
 
     scale = (2 * lat_count * LEV * LON) ** -0.5
     merge_rows = 4 * D // lat_count
@@ -575,38 +676,12 @@
     mterms[...] = term.astype(BF16).reshape(nx, nz, 2, merge_rows, 128)
     merge_sum.start()
     gather_lifted.forward()
-    mnorm.middle()
-    gather_lifted.finish()
-    up_all[tp] = dot(lifted_all[...], up_weight[...]).astype(BF16)
-    gather_up.start()
-
-    grad_mn = mnorm.finish()
-    merged_chunk, cot_chunk = [], []
-    for r in range(2):
-        for s in range(2):
-            some = pl.ds(r * ROW + s + tp * SHARE, CSHARE, stride=2)
-            merged_chunk.append(get(resid, some))
-            cot_chunk.append(get(cotf, some))
-    merged_chunk = jnp.concatenate(merged_chunk, axis=1)
-    cot_chunk = jnp.concatenate(cot_chunk, axis=1)
-    grad_merged = normalize_back(merged_chunk, gain_merge[...], grad_mn)
-    grad_quads = (cot_chunk + grad_merged).astype(BF16)
-    low = wexp[:, 0:128].reshape(TP * 128, D)
-    high = wexp[:, 64:192].reshape(TP * 128, D)
+
+    first, second = mmoments.finish()
     for s in range(2):
-        top = grad_quads[:, s * D : (s + 1) * D]
-        bottom = grad_quads[:, (2 + s) * D : (3 + s) * D]
-        put(grad_mix, pl.ds(s, CSHARE, stride=2), dot_nt(top, low) + dot_nt(bottom, high))
-        put(grad_resid, pl.ds(s, CSHARE, stride=2), top.astype(F32))
-        put(grad_resid, pl.ds(SHARE + s, CSHARE, stride=2), bottom.astype(F32))
-    grad_mix_send[...] = get(grad_mix, pl.ds(0, SHARE)).astype(BF16)
-    mix.start()
-    grad_mix_all[aligned(tp, SHARE)] = grad_mix_send[:, aligned(tp, 128)]
-    gather_up.forward()
-    merge_sum.middle()
-    mix.finish()
-
-    both = grad_mix_all[...].astype(F32)
+        inner = gheads[s].finish() - first * head_ones - second * head_unit[s]
+        put(grad_mix, pl.ds(s, CTOK, stride=2), head_cot[s] + minverse[...] * inner)
+    both = grad_mix[0]
     grad_mix_rows[0:ROW] = high_lanes(both).astype(BF16)
     grad_mix_rows[ROW : 2 * ROW] = high_lanes(pltpu.roll(both, 64, 1)).astype(BF16)
 
@@ -629,6 +704,10 @@
         back[r] = (far_a + far_b).astype(BF16)
         send_back[r].start()
         grad_other[r] = own_a + own_b
+    gather_lifted.finish()
+    up_all[tp] = dot(lifted_all[...], up_weight[...]).astype(BF16)
+    gather_up.start()
+    merge_sum.middle()
     for made in send_back:
         made.wait_recv()
     for r in range(2):
@@ -636,8 +715,8 @@
     for r in range(2):
         rows = pl.ds(r * ROW, ROW)
         part = dot(grad_q[rows], fine_w[0:128]) + dot(grad_kv[rows], fine_w[64:192])
-        gn_terms[:, :, r] = part.astype(BF16).reshape(ZH, YS, SHARE, D)
-    gnorm.start()
+        gn_terms[r] = part.astype(BF16).reshape(ZH, YS, SHARE, D)
+        gnorm[r].start()
 
     term_q = dot_tn(normed[...], grad_q[...]) * scale
     term_kv = dot_tn(normed[...], grad_kv[...]) * scale
@@ -647,8 +726,25 @@
     )
     fterms[...] = term.astype(BF16).reshape(nx, nz, 2, 2 * weight_rows, 128)
     fine_sum.start()
-    gnorm.middle()
+    gather_up.forward()
+    for part in gnorm:
+        part.middle()
     fine_sum.middle()
+
+    grad_mn = mnorm.finish()
+    merged_chunk, cot_chunk = [], []
+    for r in range(2):
+        for s in range(2):
+            some = pl.ds(r * ROW + s + tp * SHARE, CSHARE, stride=2)
+            merged_chunk.append(get(resid, some))
+            cot_chunk.append(get(cotf, some))
+    merged_chunk = jnp.concatenate(merged_chunk, axis=1)
+    cot_chunk = jnp.concatenate(cot_chunk, axis=1)
+    grad_quads = cot_chunk + normalize_back(merged_chunk, gain_merge[...], grad_mn)
+    for r in range(2):
+        for s in range(2):
+            some = grad_quads[:, (2 * r + s) * D : (2 * r + s + 1) * D]
+            put(grad_resid, pl.ds(r * SHARE + s, CSHARE, stride=2), some)
 
     gather_up.finish()
     for r in range(2):
@@ -664,19 +760,26 @@
             for block in range(TP):
                 at = r * ROW + block * SHARE + level * 8
                 pieces.append(get(resid, pl.ds(at, 8)) + get(up_wide, pl.ds(at, 8)))
-            next_fields[r, level] = jnp.concatenate(pieces, axis=0).astype(BF16)
-
-    grad_norm = gnorm.finish()
-    for r in range(2):
+            fields_out[r, level] = jnp.concatenate(pieces, axis=0).astype(BF16)
+    written = fetch(fields_out, next_fields, 6)
+
+    for r in range(2):
+        grad_norm = gnorm[r].finish()
         own_hidden = hid[pl.ds(pl.multiple_of(r * ROW + tp * SHARE, SHARE), SHARE)]
-        grad_hidden = normalize_back(own_hidden, gain_fine[...], grad_norm[r])
+        grad_hidden = normalize_back(own_hidden, gain_fine[...], grad_norm)
         grad_hidden = grad_hidden + get(grad_resid, pl.ds(r * SHARE, SHARE))
         fields_grad[r] = grad_hidden.astype(BF16)
     merge_grad[...] = merge_sum.finish()
     sums = fine_sum.finish()
     fine_grad[:, 0, 0:64] = sums[0:weight_rows, 0:64]
     fine_grad[:, 0, 64:192] = sums[weight_rows : 2 * weight_rows]
+    written.wait()
     links.finish()
+
+
+def hand_over(*refs):
+    for i in range(4):
+        refs[4 + i][...] = refs[i][...]
 
 
 def vmem(*shape, kind=BF16):
@@ -685,6 +788,19 @@
 
 def scatter_buffers(*chunk):
     return [vmem(ZH, YS, *chunk), vmem(YS - 1, ZH, *chunk), vmem(*chunk), vmem(*chunk)]
+
+
+def halved(*buffers):
+    return [vmem(2, *some.shape) for some in buffers]
+
+
+def moment_buffers():
+    return [
+        vmem(8, 128, kind=F32),
+        vmem(YS - 1, 8, 128, kind=F32),
+        vmem(8, 128, kind=F32),
+        vmem(8, 128, kind=F32),
+    ]
 
 
 def lat_buffers(nx, nz, rows):
@@ -716,10 +832,17 @@
     nz = min(8, lat_count // 4)
     nx = lat_count // (2 * nz)
     whole = pl.BlockSpec(memory_space=pltpu.VMEM)
-    copies = 160
+    left = pl.BlockSpec(memory_space=pl.ANY)
+    copies = 200
     scratch = [
         pltpu.SemaphoreType.DMA((copies,)),
         pltpu.SemaphoreType.DMA((copies,)),
+        pltpu.SemaphoreType.DMA((7,)),
+        vmem(4 * D, 128),
+        vmem(2, 192, DC),
+        vmem(DC, 256),
+        vmem(2, LEV, LON, D),
+        vmem(2, LEV, LON, D),
         vmem(2 * ROW, D, kind=F32),
         vmem(4, 2 * ROW, 128, kind=F32),
         vmem(2 * ROW, D),
@@ -744,16 +867,20 @@
         vmem(2, CTOK, 128),
         vmem(2, CTOK, 128),
         *scatter_buffers(CSHARE, DC),
-        *scatter_buffers(CSHARE, DC),
-        vmem(CSHARE, DC),
+        *scatter_buffers(CTOK, 128),
+        vmem(CTOK, DC, kind=F32),
+        vmem(CTOK, 128, kind=F32),
+        *moment_buffers(),
         vmem(CTOK, 128),
         vmem(CTOK, DC),
         *scatter_buffers(CSHARE, 4 * D),
         vmem(TP, CTOK, 256),
         vmem(4, 2 * ROW, 128, kind=F32),
-        vmem(TP, SHARE, 128, kind=F32),
-        vmem(SHARE, TP * 128),
-        vmem(ROW, 128),
+        vmem(CTOK, 4 * D, kind=F32),
+        vmem(CTOK, 128, kind=F32),
+        *moment_buffers(),
+        *halved(*scatter_buffers(CTOK, 128)),
+        vmem(1, ROW, 128, kind=F32),
         vmem(2 * ROW, 128),
         vmem(4, 2 * SHARE, 128, kind=F32),
         vmem(2 * ROW, 128),
@@ -761,11 +888,11 @@
         vmem(2, ROW, 128, kind=F32),
         vmem(2, ROW, 128),
         vmem(2, ROW, 128),
-        *scatter_buffers(2, SHARE, D),
+        *halved(*scatter_buffers(SHARE, D)),
         *lat_buffers(nx, nz, merge_rows),
         *lat_buffers(nx, nz, 2 * weight_rows),
     ]
-    next_fields, fields_grad, fine_grad, merge_grad = pl.pallas_call(
+    results = pl.pallas_call(
         functools.partial(main_kernel, lat_count, nx, nz),
         out_shape=(
             jax.ShapeDtypeStruct((2, LEV, LON, D), BF16),
@@ -773,8 +900,8 @@
             jax.ShapeDtypeStruct((weight_rows, 1, 192), F32),
             jax.ShapeDtypeStruct((merge_rows, 128), F32),
         ),
-        in_specs=[whole] * 13,
-        out_specs=[whole] * 4,
+        in_specs=[whole] * 7 + [left, whole] + [left] * 4,
+        out_specs=[left] + [whole] * 3,
         scratch_shapes=scratch,
         name="block",
         compiler_params=pltpu.CompilerParams(
@@ -795,6 +922,13 @@
         up_weight,
         cotangent,
     )
+    next_fields, fields_grad, fine_grad, merge_grad = pl.pallas_call(
+        hand_over,
+        out_shape=tuple(jax.ShapeDtypeStruct(some.shape, some.dtype) for some in results),
+        in_specs=[whole] * 4,
+        out_specs=[whole] * 4,
+        name="hand_over",
+    )(*results)
     return next_fields, fields_grad.reshape(2, LEV, LON // TP, D), fine_grad, merge_grad
 
 

time: 151 us -> 137 us (0.907)
  the two profiles are of different devices: /device:TPU:1 before, /device:TPU:100 now
where the time goes in v3:
time: 137 us
  Pallas kernels  137 us (100%)
    pallas_call x1, Pallas kernels, local(): pl.pallas_call(functools.partial(main_kernel, lat_count, nx, nz), out_sha...  135 us

profile of v3, /device:TPU:100, one launch (start us, length us, event | category | flops | bytes accessed | tf_op | source)
XLA Modules:
  0.0 137.2 jit_solution(14006342865064726941)
XLA Ops:
  0.6 134.6 %block.1 = (bf16[2,4,64,512]{3,2,1,0:T(8,128)(2,1)}, bf16[2,32,512]{2,1,0:T(8,128)(2,1)}, f32[8,1,192]{2,1,0:T(1,128)}, f32[32,128]{1,0:T(8,128)}) custom-call(bf16[2,4,64,512]{3,2,1,0:T(8,128)(2,1)} %fields.1, s32[2,64]{1,0:T(2,128)} %classes.1, bf16[8,512]{1,0:T(8,128)(2,1)} %class_table.1, f32[1,512]{1,0:T(1,128)} %bitcast.16, bf16[192,512]{1,0:T(8,128)(2,1)} %bitcast.12, ...), custom_call_target="tpu_custom_call" | custom-call | tf_op jit(solution)/shard_map/block/pallas_call | solution.py:895
  135.3 1.9 %hand_over.1 = (bf16[2,4,64,512]{3,2,1,0:T(8,128)(2,1)}, bf16[2,32,512]{2,1,0:T(8,128)(2,1)}, f32[8,1,192]{2,1,0:T(1,128)}, f32[32,128]{1,0:T(8,128)}) custom-call(bf16[2,4,64,512]{3,2,1,0:T(8,128)(2,1)} %get-tuple-element.12.refs_0_, bf16[2,32,512]{2,1,0:T(8,128)(2,1)} %get-tuple-element.13.refs_1_, f32[8,1,192]{2,1,0:T(1,128)} %get-tuple-element.14.refs_2_, ...), custom_call_target="tpu_custom_call" | custom-call | tf_op jit(solution)/shard_map/hand_over/pallas_call | solution.py:925

commit v4 on v3

--- a/solution.py
+++ b/solution.py
@@ -24,6 +24,8 @@
 CTOK = ROW // 2
 SHARE = ROW // TP
 CSHARE = CTOK // TP
+HALF = ROW // ZH
+CHALF = CTOK // ZH
 SCALE = 0.125
 
 
@@ -113,6 +115,50 @@
             made.wait_recv()
 
 
+class HalfGather:
+    def __init__(self, group, view, near):
+        links, far = group.links, 1 - near
+        sent, own, passed = view(group.tp, far), view(group.tp, near), view(group.other, near)
+        self.over_z = links.copy(sent, sent, {"tp": group.other})
+        self.over_y = [links.copy(own, own, group.along_y(k)) for k in range(1, YS)]
+        self.passed = [links.copy(passed, passed, group.along_y(k)) for k in range(1, YS)]
+
+    start, forward, finish = Gather.start, Gather.forward, Gather.finish
+
+
+class GatherY:
+    def __init__(self, group, refs):
+        self.copies = [
+            group.links.copy(some, some, group.along_y(k)) for k in range(1, YS) for some in refs
+        ]
+
+    def start(self):
+        for made in self.copies:
+            made.start()
+
+    def finish(self):
+        for made in self.copies:
+            made.wait_recv()
+
+
+class ScatterY:
+    def __init__(self, group, terms, came):
+        self.group, self.terms, self.came = group, terms, came
+        self.copies = [
+            group.links.copy(terms.at[group.y_at(k)], came.at[k - 1], group.along_y(k))
+            for k in range(1, YS)
+        ]
+
+    start, wait = GatherY.start, GatherY.finish
+
+    def finish(self):
+        self.wait()
+        total = self.terms[self.group.y].astype(F32)
+        for k in range(YS - 1):
+            total = total + self.came[k].astype(F32)
+        return total
+
+
 class Scatter:
     def __init__(self, group, terms, came_y, half, came_z):
         self.group, self.terms = group, terms
@@ -147,37 +193,29 @@
 
 
 class Moments:
-    def __init__(self, group, own, came_y, half, came_z):
-        self.own, self.came_y, self.half, self.came_z = own, came_y, half, came_z
-        links = group.links
-        self.over_y = [
-            links.copy(own, came_y.at[k - 1], group.along_y(k)) for k in range(1, YS)
+    def __init__(self, group, own, came):
+        self.own, self.came = own, came
+        self.copies = [
+            group.links.copy(own, came.at[k - 1], group.along_y(k)) for k in range(1, YS)
         ]
-        self.over_z = links.copy(half, came_z, {"tp": group.other})
 
     def start(self, inner, unit):
         first = jnp.mean(inner, axis=-1, keepdims=True)
         second = jnp.mean(inner * unit, axis=-1, keepdims=True)
-        lane = lax.broadcasted_iota(jnp.int32, (CTOK, 128), 1)
+        lane = lax.broadcasted_iota(jnp.int32, (CHALF, 128), 1)
         both = jnp.where(lane == 0, first, jnp.where(lane == 1, second, 0.0))
+        both = jnp.concatenate([both, jnp.zeros((128 - CHALF, 128), F32)], axis=0)
         self.own[...] = both.T[0:8]
-        for made in self.over_y:
+        for made in self.copies:
             made.start()
 
-    def middle(self):
-        for made in self.over_y:
-            made.wait_recv()
+    def finish(self):
         total = self.own[...]
         for k in range(YS - 1):
-            total = total + self.came_y[k]
-        self.half[...] = total
-        self.over_z.start()
-
-    def finish(self):
-        self.over_z.wait_recv()
-        total = self.half[...] + self.came_z[...]
-        both = jnp.concatenate([total, jnp.zeros((CTOK - 8, 128), F32)], axis=0).T
-        return both[:, 0:1], both[:, 1:2]
+            self.copies[k].wait_recv()
+            total = total + self.came[k]
+        both = jnp.concatenate([total, jnp.zeros((120, 128), F32)], axis=0).T
+        return both[0:CHALF, 0:1], both[0:CHALF, 1:2]
 
 
 class LatSum:
@@ -221,10 +259,79 @@
         return total
 
 
+class FarWeights:
+    def __init__(self, group, place, sources, targets):
+        links, nx, nz = group.links, place.nx, place.nz
+        mine = 2 * place.x + place.core
+        (merge, coarse), (far_merge, far_coarse) = sources, targets
+        merge_rows, coarse_rows = 4 * D // (2 * nx), 512 // (2 * nx)
+        rows, lanes = merge_rows // nz, DC // nz
+
+        def piece(refs):
+            start = pl.multiple_of(mine * merge_rows + place.z * rows, rows)
+            return [
+                refs[0].at[pl.ds(start, rows)],
+                refs[1].at[aligned(mine, coarse_rows), aligned(place.z, lanes)],
+            ]
+
+        def plane(x):
+            at = 2 * x + place.core
+            return [
+                far_merge.at[aligned(at, merge_rows)],
+                far_coarse.at[aligned(at, coarse_rows)],
+            ]
+
+        got = piece(targets)
+        self.fetched = [
+            links.copy(src, dst, {"tp": group.other}) for src, dst in zip(piece(sources), got)
+        ]
+        self.along_z = [
+            links.copy(some, some, place.at(place.x, z, place.core))
+            for z in place.z_peers
+            for some in got
+        ]
+        self.along_x = [
+            links.copy(some, some, place.at(x, place.z, core))
+            for x, core in place.x_peers[1::2]
+            for some in plane(place.x)
+        ]
+        self.to_twin = [
+            links.copy(some, some, place.at(place.x, place.z, 1 - place.core))
+            for x in range(nx)
+            for some in plane(x)
+        ]
+
+    def start(self):
+        for made in self.fetched:
+            made.start()
+
+    def pass_z(self):
+        for made in self.fetched:
+            made.wait_recv()
+        for made in self.along_z:
+            made.start()
+
+    def pass_x(self):
+        for made in self.along_z:
+            made.wait_recv()
+        for made in self.along_x:
+            made.start()
+
+    def pass_core(self):
+        for made in self.along_x:
+            made.wait_recv()
+        for made in self.to_twin:
+            made.start()
+
+    def finish(self, which):
+        for made in self.to_twin[which::2]:
+            made.wait_recv()
+
+
 class Place:
     def __init__(self, nx, nz):
         lat = lax.axis_index("lat")
-        self.nz = nz
+        self.nx, self.nz = nx, nz
         self.core = lax.rem(lat, 2)
         self.z = lax.rem(lax.div(lat, 2), nz)
         self.x = lax.div(lat, 2 * nz)
@@ -315,7 +422,9 @@
     recv_sems,
     local_sems,
     merge_weight,
-    coarse_w,
+    own_coarse,
+    far_merge,
+    far_coarse,
     up_weight,
     cotangent,
     fields_out,
@@ -347,37 +456,29 @@
     cback_came,
     cs_terms,
     cs_y,
-    cs_half,
-    cs_z,
     cn_terms,
     cn_y,
-    cn_half,
-    cn_z,
     cunit,
     cinverse,
     cm_own,
     cm_y,
-    cm_half,
-    cm_z,
     grad_columns,
+    far_columns,
     lifted_all,
     mn_terms,
     mn_y,
-    mn_half,
-    mn_z,
     up_all,
     up_wide,
     munit,
     minverse,
     mm_own,
     mm_y,
-    mm_half,
-    mm_z,
     gh_terms,
     gh_y,
-    gh_half,
-    gh_z,
+    mix_sent,
+    mix_came,
     grad_mix,
+    mix_all,
     grad_mix_rows,
     grad_resid,
     grad_q,
@@ -406,10 +507,11 @@
     got_cotangent = fetch(cotangent_in, cotangent, 0)
     got_up = fetch(up_weight_in, up_weight, 1)
     got_merge = fetch(merge_weight_in, merge_weight, 2)
-    got_coarse = [fetch(coarse_w_in, coarse_w, 3)]
-    for head in range(2):
-        rows = coarse_out_in.at[pl.ds(64 * head, 64)]
-        got_coarse.append(fetch(rows, cexp.at[head, pl.ds(64, 64)], 4 + head))
+    got_coarse = [
+        fetch(coarse_w_in.at[0], own_coarse.at[pl.ds(0, 192)], 3),
+        fetch(coarse_w_in.at[1], own_coarse.at[pl.ds(192, 192)], 4),
+        fetch(coarse_out_in, own_coarse.at[pl.ds(384, 128)], 5),
+    ]
 
     links = Links(send_sems, recv_sems)
     group = Group(links)
@@ -434,7 +536,7 @@
     wexp[:, 0:64] = blank
     wexp[:, 128:192] = blank
     wexp[tp, 64:128] = fine_out[...]
-    for head in range(2):
+    for head in range(4):
         cexp[head, 0:64] = jnp.zeros((64, DC), BF16)
 
     gather_w = Gather(group, lambda at: wexp.at[at, pl.ds(64, 64)])
@@ -443,24 +545,31 @@
         links.copy(keys_sent.at[1], keys_came.at[0], {"lat": after}),
         links.copy(keys_sent.at[0], keys_came.at[1], {"lat": before}),
     ]
-    gather_heads = [
-        Gather(group, lambda at, i=i: heads_all.at[pl.ds(i * 128, 128), aligned(at, 128)])
-        for i in range(2)
-    ]
-    gather_lift = Gather(group, lambda at: lift_all.at[aligned(at, CSHARE)])
-    gather_coarse = Gather(group, lambda at: coarse_all.at[:, aligned(at, 128)])
+    zh, other = group.zh, group.other
+    far_half = 1 - zh
+
+    def head_slot(at, half):
+        return heads_all.at[aligned(half, HALF), aligned(at, 128)]
+
+    near_heads = HalfGather(group, head_slot, zh)
+    far_heads = HalfGather(group, head_slot, far_half)
+    gather_lift = GatherY(group, [lift_all.at[aligned(group.y, CSHARE)]])
+    gather_coarse = GatherY(
+        group, [coarse_all.at[:, aligned(tp, 128)], coarse_all.at[:, aligned(other, 128)]]
+    )
+    far = FarWeights(group, place, (merge_weight, own_coarse), (far_merge, far_coarse))
     send_ckeys = links.copy(ckeys, ckeys_came, {"lat": twin})
     send_cback = links.copy(cback, cback_came, {"lat": twin})
-    csum = Scatter(group, cs_terms, cs_y, cs_half, cs_z)
-    cnorm = Scatter(group, cn_terms, cn_y, cn_half, cn_z)
-    cmoments = Moments(group, cm_own, cm_y, cm_half, cm_z)
+    csum = ScatterY(group, cs_terms, cs_y)
+    cnorm = ScatterY(group, cn_terms, cn_y)
+    cmoments = Moments(group, cm_own, cm_y)
+    swap_columns = links.copy(grad_columns.at[far_half], far_columns, {"tp": other})
     gather_lifted = Gather(group, lambda at: lifted_all.at[aligned(at, CSHARE)])
-    mnorm = Scatter(group, mn_terms, mn_y, mn_half, mn_z)
+    mnorm = ScatterY(group, mn_terms, mn_y)
     gather_up = Gather(group, lambda at: up_all.at[at])
-    mmoments = Moments(group, mm_own, mm_y, mm_half, mm_z)
-    gheads = [
-        Scatter(group, gh_terms.at[s], gh_y.at[s], gh_half.at[s], gh_z.at[s]) for s in range(2)
-    ]
+    mmoments = Moments(group, mm_own, mm_y)
+    gheads = [ScatterY(group, gh_terms.at[z], gh_y.at[z]) for z in (far_half, zh)]
+    swap_mix = links.copy(mix_sent, mix_came, {"tp": other})
     send_back = [
         links.copy(back.at[0], back_came.at[1], {"lat": before}),
         links.copy(back.at[1], back_came.at[0], {"lat": after}),
@@ -498,6 +607,10 @@
     for made in send_keys:
         made.start()
     gather_w.start()
+    got_merge.wait()
+    for made in got_coarse:
+        made.wait()
+    far.start()
 
     got_cotangent.wait()
     got_up.wait()
@@ -512,6 +625,7 @@
     quad = jnp.where(lax.rem(tp, 2) == 0, quad[:, 0:256], quad[:, 256:512]).astype(BF16)
     lift_terms[...] = dot_nt(quad, up_weight[...]).astype(BF16).reshape(ZH, YS, CSHARE, DC)
     lift.start()
+    far.pass_z()
 
     for made in send_keys:
         made.wait_recv()
@@ -538,150 +652,173 @@
     lane = lax.broadcasted_iota(jnp.int32, (ROW, 128), 1)
     packed = jnp.where(lane < 64, pltpu.roll(mixture[ROW : 2 * ROW], 64, 1), mixture[0:ROW])
     heads_all[:, aligned(tp, 128)] = packed.astype(BF16)
-    for part in gather_heads:
-        part.over_z.start()
-    for part in gather_heads:
-        for made in part.over_y:
-            made.start()
+    near_heads.start()
+    far_heads.start()
 
     lift.middle()
+    far.pass_x()
     gather_w.finish()
-    for part in gather_heads:
-        part.forward()
+    near_heads.forward()
     lift_chunk = lift.finish().astype(BF16)
-    lift_all[aligned(tp, CSHARE)] = lift_chunk
+    lift_all[aligned(group.y, CSHARE)] = lift_chunk
     gather_lift.start()
-    for part in gather_heads:
-        part.finish()
-
-    for r in range(2):
-        first = 64 if r == 1 else 0
-        weight = wexp[:, first : first + 128].reshape(TP * 128, D)
-        rows = pl.ds(r * ROW, ROW)
-        put(resid, rows, hid[rows] + dot(heads_all[...], weight))
-
-    merged = [get(resid, pl.ds(r * ROW + s, CTOK, stride=2)) for r in range(2) for s in range(2)]
-    merged = jnp.concatenate(merged, axis=1)
-    unit, inverse = standardize(merged)
-    merged_norm[...] = (unit * gain_merge[...]).astype(BF16)
-    got_merge.wait()
-    coarse_all[:, aligned(tp, 128)] = dot(merged_norm[...], merge_weight[...]).astype(BF16)
+    far.pass_core()
+    far_heads.forward()
+    near_heads.finish()
+
+    low = wexp[:, 0:128].reshape(TP * 128, D)
+    high = wexp[:, 64:192].reshape(TP * 128, D)
+
+    def merge(half):
+        for r, weight in ((0, low), (1, high)):
+            rows = pl.ds(pl.multiple_of(r * ROW + half * HALF, HALF), HALF)
+            put(resid, rows, hid[rows] + dot(heads_all[aligned(half, HALF)], weight))
+        quads = [
+            get(resid, pl.ds(r * ROW + half * HALF + s, CHALF, stride=2))
+            for r in range(2)
+            for s in range(2)
+        ]
+        unit, inverse = standardize(jnp.concatenate(quads, axis=1))
+        merged_norm[aligned(half, CHALF)] = (unit * gain_merge[...]).astype(BF16)
+        return unit, inverse
+
+    unit, inverse = merge(zh)
+    near_merged = merged_norm[aligned(zh, CHALF)]
+    coarse_all[:, aligned(tp, 128)] = dot(near_merged, merge_weight[...]).astype(BF16)
+    far.finish(0)
+    coarse_all[:, aligned(other, 128)] = dot(near_merged, far_merge[...]).astype(BF16)
     gather_coarse.start()
     munit[...] = unit
-    minverse[...] = jnp.broadcast_to(inverse, (CTOK, 128))
-    gather_lift.forward()
-    gather_coarse.forward()
+    minverse[...] = jnp.broadcast_to(inverse, (CHALF, 128))
+    far.finish(1)
     gather_lift.finish()
-    for made in got_coarse:
-        made.wait()
-    grad_cmix = [dot_nt(lift_all[...], cexp[head]).astype(BF16) for head in range(2)]
+    stacks = [(own_coarse, 0), (own_coarse, 1), (far_coarse, 0), (far_coarse, 1)]
+    for head, (stack, at) in enumerate(stacks):
+        cexp[head, 64:128] = stack[384 + 64 * at : 448 + 64 * at]
+    grad_cmix = [dot_nt(lift_all[...], cexp[head]).astype(BF16) for head in range(4)]
     gather_coarse.finish()
 
     coarse_f[...] = coarse_all[...].astype(F32)
     unit, inverse = standardize(coarse_f[...])
     cnormed = (unit * gain_coarse[...]).astype(BF16)
-    for head in range(2):
-        ckeys[head] = dot_nt(cnormed, coarse_w[head, 64:192]).astype(BF16)
+    for head, (stack, at) in enumerate(stacks):
+        rows = stack[192 * at + 64 : 192 * at + 192]
+        ckeys[head] = dot_nt(cnormed, rows).astype(BF16)
     send_ckeys.start()
     cunit[...] = unit
-    cinverse[...] = jnp.broadcast_to(inverse, (CTOK, 128))
-    cq = [low_lanes(dot_nt(cnormed, coarse_w[head, 0:128])).astype(BF16) for head in range(2)]
-
-    row_at = lax.broadcasted_iota(jnp.int32, (CTOK, CTOK), 0)
-    col_at = lax.broadcasted_iota(jnp.int32, (CTOK, CTOK), 1)
+    cinverse[...] = jnp.broadcast_to(inverse, (CHALF, 128))
+    cq = [
+        low_lanes(dot_nt(cnormed, stack[192 * at : 192 * at + 128])).astype(BF16)
+        for stack, at in stacks
+    ]
+
+    row_at = lax.broadcasted_iota(jnp.int32, (CHALF, CHALF), 0)
+    col_at = lax.broadcasted_iota(jnp.int32, (CHALF, CHALF), 1)
     cmask = (row_at >> 5) == (col_at >> 5)
     own_scores = [
-        jnp.where(cmask, dot_nt(cq[head], ckeys[head]) * SCALE, NEGATIVE) for head in range(2)
+        jnp.where(cmask, dot_nt(cq[head], ckeys[head]) * SCALE, NEGATIVE) for head in range(4)
     ]
     send_ckeys.wait_recv()
     cgrad_q, cgrad_kv = [], []
     cheads = []
-    for head in range(2):
-        far = jnp.where(cmask, dot_nt(cq[head], ckeys_came[head]) * SCALE, NEGATIVE)
-        own, far = softmax_pair(own_scores[head], far)
-        own16, far16 = own.astype(BF16), far.astype(BF16)
+    for head in range(4):
+        away = jnp.where(cmask, dot_nt(cq[head], ckeys_came[head]) * SCALE, NEGATIVE)
+        own, away = softmax_pair(own_scores[head], away)
+        own16, far16 = own.astype(BF16), away.astype(BF16)
         grad_own = dot_nt(grad_cmix[head], ckeys[head])
         grad_far = dot_nt(grad_cmix[head], ckeys_came[head])
-        ds_own, ds_far = score_grads(own, far, grad_own, grad_far)
+        ds_own, ds_far = score_grads(own, away, grad_own, grad_far)
         cback[head] = (dot_tn(ds_far, cq[head]) + dot_tn(far16, grad_cmix[head])).astype(BF16)
         cgrad_kv.append(dot_tn(ds_own, cq[head]) + dot_tn(own16, grad_cmix[head]))
         query_grad = dot(ds_own, ckeys[head]) + dot(ds_far, ckeys_came[head])
         cgrad_q.append(low_lanes(query_grad).astype(BF16))
         cheads.append((dot(own16, ckeys[head]) + dot(far16, ckeys_came[head])).astype(BF16))
     send_cback.start()
-    part = dot(cheads[0], cexp[0]) + dot(cheads[1], cexp[1])
-    cs_terms[...] = part.astype(BF16).reshape(ZH, YS, CSHARE, DC)
-    csum.start()
-    part = dot(cgrad_q[0], coarse_w[0, 0:128]) + dot(cgrad_q[1], coarse_w[1, 0:128])
+    part = sum(dot(cheads[head], cexp[head]) for head in range(4))
+    cs_terms[...] = part.astype(BF16).reshape(YS, CSHARE, DC)
+    part = 0.0
+    for head, (stack, at) in enumerate(stacks):
+        part = part + dot(cgrad_q[head], stack[192 * at : 192 * at + 128])
     send_cback.wait_recv()
-    for head in range(2):
+    for head, (stack, at) in enumerate(stacks):
         total = (cgrad_kv[head] + cback_came[head].astype(F32)).astype(BF16)
-        part = part + dot(total, coarse_w[head, 64:192])
+        part = part + dot(total, stack[192 * at + 64 : 192 * at + 192])
     for t in range(TP):
-        cn_terms[t // YS, t % YS] = part[:, 128 * t : 128 * t + 128].astype(BF16)
+        cn_terms[t % YS, t // YS] = part[:, 128 * t : 128 * t + 128].astype(BF16)
     cnorm.start()
     cmoments.start(part * gain_coarse[...], cunit[...])
-
-    own_low, own_high = wexp[tp, 0:128], wexp[tp, 64:192]
-
-    def own_head(top, bottom):
-        return dot_nt(top.astype(BF16), own_low) + dot_nt(bottom.astype(BF16), own_high)
-
-    head_cot, head_unit = [], []
-    for s in range(2):
-        top, bottom = [get(cotf, pl.ds(r * ROW + s, CTOK, stride=2)) for r in range(2)]
-        head_cot.append(own_head(top, bottom))
-        top, bottom = [munit[:, (2 * r + s) * D : (2 * r + s + 1) * D] for r in range(2)]
-        head_unit.append(own_head(top, bottom))
+    csum.start()
+
+    def one_head(at, top, bottom):
+        top, bottom = top.astype(BF16), bottom.astype(BF16)
+        return dot_nt(top, wexp[at, 0:128]) + dot_nt(bottom, wexp[at, 64:192])
+
     ones = jnp.ones((8, D), BF16)
-    head_ones = own_head(ones, ones)[0:1]
-
-    cnorm.middle()
-    cmoments.middle()
-    csum.middle()
-
-    lane_block = aligned(tp, 128)
-    inner = cnorm.finish() * gain_coarse[:, lane_block]
+    head_terms = []
+    for at in (other, tp):
+        terms = []
+        for s in range(2):
+            cot = [get(cotf, pl.ds(r * ROW + zh * HALF + s, CHALF, stride=2)) for r in range(2)]
+            unit = [munit[:, (2 * r + s) * D : (2 * r + s + 1) * D] for r in range(2)]
+            terms.append((one_head(at, *cot), one_head(at, *unit)))
+        head_terms.append((terms, one_head(at, ones, ones)[0:1]))
+
+    grad_cn = cnorm.finish()
     first, second = cmoments.finish()
-    inner = cinverse[...] * (inner - first - cunit[:, lane_block] * second)
-    grad_columns[...] = (lift_all[:, lane_block].astype(F32) + inner).astype(BF16)
-
-    part = dot_nt(grad_columns[...], merge_weight[...])
+    for zc in range(ZH):
+        lane_block = aligned(zc * YS + group.y, 128)
+        inner = grad_cn[zc] * gain_coarse[:, lane_block]
+        inner = cinverse[...] * (inner - first - cunit[:, lane_block] * second)
+        grad_columns[zc] = (lift_all[:, lane_block].astype(F32) + inner).astype(BF16)
+
+    part = dot_nt(grad_columns[zh], merge_weight[...])
+    part = part + dot_nt(grad_columns[far_half], far_merge[...])
     inner = part * gain_merge[...]
     inner16 = inner.astype(BF16)
-    low = wexp[:, 0:128].reshape(TP * 128, D)
-    high = wexp[:, 64:192].reshape(TP * 128, D)
     for s in range(2):
         top, bottom = [inner16[:, (2 * r + s) * D : (2 * r + s + 1) * D] for r in range(2)]
         heads = (dot_nt(top, low) + dot_nt(bottom, high)).astype(BF16)
         for t in range(TP):
-            gh_terms[s, t // YS, t % YS] = heads[:, 128 * t : 128 * t + 128]
-        gheads[s].start()
+            some = heads[:, 128 * t : 128 * t + 128]
+            gh_terms[t // YS, t % YS, s * CHALF : (s + 1) * CHALF] = some
+    for part_sum in gheads:
+        part_sum.start()
     mmoments.start(inner, munit[...])
-    mn_terms[...] = part.astype(BF16).reshape(ZH, YS, CSHARE, 4 * D)
+    swap_columns.start()
+    mn_terms[...] = part.astype(BF16).reshape(YS, CSHARE, 4 * D)
     mnorm.start()
 
     mine = aligned(tp, CSHARE)
-    lifted_all[mine] = (coarse_f[mine] + csum.finish()).astype(BF16)
-    for part in gheads:
-        part.middle()
-    mmoments.middle()
+    near_mine = aligned(group.y, CSHARE)
+    lifted_all[mine] = (coarse_f[near_mine] + csum.finish()).astype(BF16)
+
+    first, second = mmoments.finish()
+    for i, (terms, head_ones) in enumerate(head_terms):
+        grad_heads = gheads[i].finish()
+        for s in range(2):
+            head_cot, head_unit = terms[s]
+            inner = grad_heads[s * CHALF : (s + 1) * CHALF] - first * head_ones - second * head_unit
+            put(grad_mix, pl.ds(s, CHALF, stride=2), head_cot + minverse[...] * inner)
+        if i == 0:
+            mix_sent[...] = grad_mix[0].astype(BF16)
+            swap_mix.start()
+    mix_all[aligned(zh, HALF)] = grad_mix[0]
     gather_lifted.start()
-    mnorm.middle()
-
+
+    far_heads.finish()
+    merge(far_half)
+    swap_columns.wait_recv()
     scale = (2 * lat_count * LEV * LON) ** -0.5
     merge_rows = 4 * D // lat_count
     weight_rows = D // lat_count
-    term = dot_tn(merged_norm[...], grad_columns[...]) * scale
-    mterms[...] = term.astype(BF16).reshape(nx, nz, 2, merge_rows, 128)
+    term = dot_tn(merged_norm[aligned(zh, CHALF)], grad_columns[zh])
+    term = term + dot_tn(merged_norm[aligned(far_half, CHALF)], far_columns[...])
+    mterms[...] = (term * scale).astype(BF16).reshape(nx, nz, 2, merge_rows, 128)
+    swap_mix.wait_recv()
+    mix_all[aligned(far_half, HALF)] = mix_came[...].astype(F32)
     merge_sum.start()
     gather_lifted.forward()
-
-    first, second = mmoments.finish()
-    for s in range(2):
-        inner = gheads[s].finish() - first * head_ones - second * head_unit[s]
-        put(grad_mix, pl.ds(s, CTOK, stride=2), head_cot[s] + minverse[...] * inner)
-    both = grad_mix[0]
+    both = mix_all[...]
     grad_mix_rows[0:ROW] = high_lanes(both).astype(BF16)
     grad_mix_rows[ROW : 2 * ROW] = high_lanes(pltpu.roll(both, 64, 1)).astype(BF16)
 
@@ -794,13 +931,12 @@
     return [vmem(2, *some.shape) for some in buffers]
 
 
+def y_buffers(*chunk):
+    return [vmem(YS, *chunk), vmem(YS - 1, *chunk)]
+
+
 def moment_buffers():
-    return [
-        vmem(8, 128, kind=F32),
-        vmem(YS - 1, 8, 128, kind=F32),
-        vmem(8, 128, kind=F32),
-        vmem(8, 128, kind=F32),
-    ]
+    return [vmem(8, 128, kind=F32), vmem(YS - 1, 8, 128, kind=F32)]
 
 
 def lat_buffers(nx, nz, rows):
@@ -833,13 +969,15 @@
     nx = lat_count // (2 * nz)
     whole = pl.BlockSpec(memory_space=pltpu.VMEM)
     left = pl.BlockSpec(memory_space=pl.ANY)
-    copies = 200
+    copies = 240
     scratch = [
         pltpu.SemaphoreType.DMA((copies,)),
         pltpu.SemaphoreType.DMA((copies,)),
         pltpu.SemaphoreType.DMA((7,)),
         vmem(4 * D, 128),
-        vmem(2, 192, DC),
+        vmem(512, DC),
+        vmem(4 * D, 128),
+        vmem(512, DC),
         vmem(DC, 256),
         vmem(2, LEV, LON, D),
         vmem(2, LEV, LON, D),
@@ -855,32 +993,36 @@
         vmem(2 * ROW, 128, kind=F32),
         vmem(ROW, TP * 128),
         vmem(TP, 192, D),
-        vmem(2, 128, DC),
+        vmem(4, 128, DC),
         vmem(4, 2 * ROW, 128, kind=F32),
         vmem(CTOK, 4 * D),
+        vmem(CHALF, DC),
+        vmem(CHALF, DC, kind=F32),
+        vmem(CHALF, DC),
+        *scatter_buffers(CSHARE, DC),
+        vmem(4, CHALF, 128),
+        vmem(4, CHALF, 128),
+        vmem(4, CHALF, 128),
+        vmem(4, CHALF, 128),
+        *y_buffers(CSHARE, DC),
+        *y_buffers(ZH, CHALF, 128),
+        vmem(CHALF, DC, kind=F32),
+        vmem(CHALF, 128, kind=F32),
+        *moment_buffers(),
+        vmem(ZH, CHALF, 128),
+        vmem(CHALF, 128),
         vmem(CTOK, DC),
-        vmem(CTOK, DC, kind=F32),
-        vmem(CTOK, DC),
-        *scatter_buffers(CSHARE, DC),
-        vmem(2, CTOK, 128),
-        vmem(2, CTOK, 128),
-        vmem(2, CTOK, 128),
-        vmem(2, CTOK, 128),
-        *scatter_buffers(CSHARE, DC),
-        *scatter_buffers(CTOK, 128),
-        vmem(CTOK, DC, kind=F32),
-        vmem(CTOK, 128, kind=F32),
-        *moment_buffers(),
-        vmem(CTOK, 128),
-        vmem(CTOK, DC),
-        *scatter_buffers(CSHARE, 4 * D),
+        *y_buffers(CSHARE, 4 * D),
         vmem(TP, CTOK, 256),
         vmem(4, 2 * ROW, 128, kind=F32),
-        vmem(CTOK, 4 * D, kind=F32),
-        vmem(CTOK, 128, kind=F32),
+        vmem(CHALF, 4 * D, kind=F32),
+        vmem(CHALF, 128, kind=F32),
         *moment_buffers(),
-        *halved(*scatter_buffers(CTOK, 128)),
-        vmem(1, ROW, 128, kind=F32),
+        *halved(*y_buffers(2 * CHALF, 128)),
+        vmem(HALF, 128),
+        vmem(HALF, 128),
+        vmem(1, HALF, 128, kind=F32),
+        vmem(ROW, 128, kind=F32),
         vmem(2 * ROW, 128),
         vmem(4, 2 * SHARE, 128, kind=F32),
         vmem(2 * ROW, 128),

time: 137 us -> 122 us (0.89)
  the two profiles are of different devices: /device:TPU:100 before, /device:TPU:1 now
where the time goes in v4:
time: 122 us
  Pallas kernels  121 us (99%)
    pallas_call x1, Pallas kernels, local(): pl.pallas_call(functools.partial(main_kernel, lat_count, nx, nz), out_sha...  120 us

profile of v4, /device:TPU:1, one launch (start us, length us, event | category | flops | bytes accessed | tf_op | source)
XLA Modules:
  0.0 122.1 jit_solution(9858075671969501026)
XLA Ops:
  0.6 119.5 %block.1 = (bf16[2,4,64,512]{3,2,1,0:T(8,128)(2,1)}, bf16[2,32,512]{2,1,0:T(8,128)(2,1)}, f32[8,1,192]{2,1,0:T(1,128)}, f32[32,128]{1,0:T(8,128)}) custom-call(bf16[2,4,64,512]{3,2,1,0:T(8,128)(2,1)} %fields.1, s32[2,64]{1,0:T(2,128)} %classes.1, bf16[8,512]{1,0:T(8,128)(2,1)} %class_table.1, f32[1,512]{1,0:T(1,128)} %bitcast.16, bf16[192,512]{1,0:T(8,128)(2,1)} %bitcast.12, ...), custom_call_target="tpu_custom_call" | custom-call | tf_op jit(solution)/shard_map/block/pallas_call | solution.py:1037
  120.2 1.9 %hand_over.1 = (bf16[2,4,64,512]{3,2,1,0:T(8,128)(2,1)}, bf16[2,32,512]{2,1,0:T(8,128)(2,1)}, f32[8,1,192]{2,1,0:T(1,128)}, f32[32,128]{1,0:T(8,128)}) custom-call(bf16[2,4,64,512]{3,2,1,0:T(8,128)(2,1)} %get-tuple-element.12.refs_0_, bf16[2,32,512]{2,1,0:T(8,128)(2,1)} %get-tuple-element.13.refs_1_, f32[8,1,192]{2,1,0:T(1,128)} %get-tuple-element.14.refs_2_, ...), custom_call_target="tpu_custom_call" | custom-call | tf_op jit(solution)/shard_map/hand_over/pallas_call | solution.py:1067

commit v5 on v4

--- a/solution.py
+++ b/solution.py
@@ -124,6 +124,38 @@
         self.passed = [links.copy(passed, passed, group.along_y(k)) for k in range(1, YS)]
 
     start, forward, finish = Gather.start, Gather.forward, Gather.finish
+
+
+class OutGather:
+    def __init__(self, group, place, wexp):
+        links, rows = group.links, 64 // place.nx
+
+        def piece(at, x, core):
+            return wexp.at[at, pl.ds(64 + x * rows, rows), aligned(core, 256)]
+
+        def slot(at):
+            return wexp.at[at, pl.ds(64, 64)]
+
+        own, far = slot(group.tp), slot(group.other)
+        sent = piece(group.tp, place.x, place.core)
+        got = piece(group.other, place.x, place.core)
+        self.over_z = links.copy(sent, sent, {"tp": group.other, **place.mirror})
+        self.over_y = [links.copy(own, own, group.along_y(k)) for k in range(1, YS)]
+        self.shared = [links.copy(got, got, place.at(x, place.z, c)) for x, c in place.x_peers]
+        self.passed = [links.copy(far, far, group.along_y(k)) for k in range(1, YS)]
+
+    def share(self):
+        self.over_z.wait_recv()
+        for made in self.shared:
+            made.start()
+
+    def forward(self):
+        for made in self.shared:
+            made.wait_recv()
+        for made in self.passed:
+            made.start()
+
+    start, finish = Gather.start, Gather.finish
 
 
 class GatherY:
@@ -267,11 +299,11 @@
         merge_rows, coarse_rows = 4 * D // (2 * nx), 512 // (2 * nx)
         rows, lanes = merge_rows // nz, DC // nz
 
-        def piece(refs):
-            start = pl.multiple_of(mine * merge_rows + place.z * rows, rows)
+        def piece(refs, z):
+            start = pl.multiple_of(mine * merge_rows + z * rows, rows)
             return [
                 refs[0].at[pl.ds(start, rows)],
-                refs[1].at[aligned(mine, coarse_rows), aligned(place.z, lanes)],
+                refs[1].at[aligned(mine, coarse_rows), aligned(z, lanes)],
             ]
 
         def plane(x):
@@ -281,24 +313,26 @@
                 far_coarse.at[aligned(at, coarse_rows)],
             ]
 
-        got = piece(targets)
+        got = piece(targets, place.z)
+        away = nz - 1 - place.z
         self.fetched = [
-            links.copy(src, dst, {"tp": group.other}) for src, dst in zip(piece(sources), got)
+            links.copy(src, dst, {"tp": group.other, **place.mirror})
+            for src, dst in zip(piece(sources, away), piece(targets, away))
         ]
         self.along_z = [
             links.copy(some, some, place.at(place.x, z, place.core))
+            for some in got
             for z in place.z_peers
-            for some in got
         ]
         self.along_x = [
             links.copy(some, some, place.at(x, place.z, core))
+            for some in plane(place.x)
             for x, core in place.x_peers[1::2]
-            for some in plane(place.x)
         ]
         self.to_twin = [
-            links.copy(some, some, place.at(place.x, place.z, 1 - place.core))
+            links.copy(plane(x)[which], plane(x)[which], place.at(place.x, place.z, 1 - place.core))
+            for which in range(2)
             for x in range(nx)
-            for some in plane(x)
         ]
 
     def start(self):
@@ -306,25 +340,27 @@
             made.start()
 
     def pass_z(self):
-        for made in self.fetched:
-            made.wait_recv()
-        for made in self.along_z:
-            made.start()
+        self.step(self.fetched, self.along_z)
+
+    def half(self, copies, which):
+        count = len(copies) // 2
+        return copies[which * count : (which + 1) * count]
+
+    def step(self, before, then):
+        for which in range(2):
+            for made in self.half(before, which):
+                made.wait_recv()
+            for made in self.half(then, which):
+                made.start()
 
     def pass_x(self):
-        for made in self.along_z:
-            made.wait_recv()
-        for made in self.along_x:
-            made.start()
+        self.step(self.along_z, self.along_x)
 
     def pass_core(self):
-        for made in self.along_x:
-            made.wait_recv()
-        for made in self.to_twin:
-            made.start()
+        self.step(self.along_x, self.to_twin)
 
     def finish(self, which):
-        for made in self.to_twin[which::2]:
+        for made in self.half(self.to_twin, which):
             made.wait_recv()
 
 
@@ -341,6 +377,7 @@
             for j in range(2)
             if i or j
         ]
+        self.mirror = self.at(self.x, nz - 1 - self.z, self.core)
         self.z_peers = [lax.rem(self.z + k, nz) for k in range(1, nz)]
 
     def at(self, x, z, core):
@@ -529,6 +566,7 @@
     lat_peers = [{"lat": before}, {"lat": after}]
     lat_peers += [place.at(x, place.z, core) for x, core in place.x_peers]
     lat_peers += [place.at(place.x, z, place.core) for z in place.z_peers]
+    lat_peers.append({"tp": group.other, **place.mirror})
     for peer in lat_peers:
         pl.semaphore_signal(barrier, inc=1, device_id=peer, device_id_type=MESH)
 
@@ -539,7 +577,7 @@
     for head in range(4):
         cexp[head, 0:64] = jnp.zeros((64, DC), BF16)
 
-    gather_w = Gather(group, lambda at: wexp.at[at, pl.ds(64, 64)])
+    gather_w = OutGather(group, place, wexp)
     lift = Scatter(group, lift_terms, lift_y, lift_half, lift_z)
     send_keys = [
         links.copy(keys_sent.at[1], keys_came.at[0], {"lat": after}),
@@ -604,13 +642,13 @@
         keys_sent[r] = kv
 
     pl.semaphore_wait(barrier, TP - 1 + len(lat_peers))
-    for made in send_keys:
-        made.start()
-    gather_w.start()
     got_merge.wait()
     for made in got_coarse:
         made.wait()
     far.start()
+    for made in send_keys:
+        made.start()
+    gather_w.start()
 
     got_cotangent.wait()
     got_up.wait()
@@ -629,7 +667,7 @@
 
     for made in send_keys:
         made.wait_recv()
-    gather_w.forward()
+    gather_w.share()
 
     present = (lat > 0, lat < lat_count - 1)
 
@@ -653,18 +691,17 @@
     packed = jnp.where(lane < 64, pltpu.roll(mixture[ROW : 2 * ROW], 64, 1), mixture[0:ROW])
     heads_all[:, aligned(tp, 128)] = packed.astype(BF16)
     near_heads.start()
-    far_heads.start()
+    gather_w.forward()
+    far.pass_x()
 
     lift.middle()
-    far.pass_x()
-    gather_w.finish()
     near_heads.forward()
     lift_chunk = lift.finish().astype(BF16)
     lift_all[aligned(group.y, CSHARE)] = lift_chunk
     gather_lift.start()
     far.pass_core()
-    far_heads.forward()
     near_heads.finish()
+    gather_w.finish()
 
     low = wexp[:, 0:128].reshape(TP * 128, D)
     high = wexp[:, 64:192].reshape(TP * 128, D)
@@ -688,6 +725,7 @@
     far.finish(0)
     coarse_all[:, aligned(other, 128)] = dot(near_merged, far_merge[...]).astype(BF16)
     gather_coarse.start()
+    far_heads.start()
     munit[...] = unit
     minverse[...] = jnp.broadcast_to(inverse, (CHALF, 128))
     far.finish(1)
@@ -748,6 +786,7 @@
     cnorm.start()
     cmoments.start(part * gain_coarse[...], cunit[...])
     csum.start()
+    far_heads.forward()
 
     def one_head(at, top, bottom):
         top, bottom = top.astype(BF16), bottom.astype(BF16)
@@ -791,6 +830,7 @@
     mine = aligned(tp, CSHARE)
     near_mine = aligned(group.y, CSHARE)
     lifted_all[mine] = (coarse_f[near_mine] + csum.finish()).astype(BF16)
+    gather_lifted.start()
 
     first, second = mmoments.finish()
     for i, (terms, head_ones) in enumerate(head_terms):
@@ -803,7 +843,7 @@
             mix_sent[...] = grad_mix[0].astype(BF16)
             swap_mix.start()
     mix_all[aligned(zh, HALF)] = grad_mix[0]
-    gather_lifted.start()
+    gather_lifted.forward()
 
     far_heads.finish()
     merge(far_half)
@@ -814,10 +854,12 @@
     term = dot_tn(merged_norm[aligned(zh, CHALF)], grad_columns[zh])
     term = term + dot_tn(merged_norm[aligned(far_half, CHALF)], far_columns[...])
     mterms[...] = (term * scale).astype(BF16).reshape(nx, nz, 2, merge_rows, 128)
+    gather_lifted.finish()
+    up_all[tp] = dot(lifted_all[...], up_weight[...]).astype(BF16)
     swap_mix.wait_recv()
     mix_all[aligned(far_half, HALF)] = mix_came[...].astype(F32)
+    gather_up.start()
     merge_sum.start()
-    gather_lifted.forward()
     both = mix_all[...]
     grad_mix_rows[0:ROW] = high_lanes(both).astype(BF16)
     grad_mix_rows[ROW : 2 * ROW] = high_lanes(pltpu.roll(both, 64, 1)).astype(BF16)
@@ -841,9 +883,6 @@
         back[r] = (far_a + far_b).astype(BF16)
         send_back[r].start()
         grad_other[r] = own_a + own_b
-    gather_lifted.finish()
-    up_all[tp] = dot(lifted_all[...], up_weight[...]).astype(BF16)
-    gather_up.start()
     merge_sum.middle()
     for made in send_back:
         made.wait_recv()

time: 122 us -> 110 us (0.902)
  the two profiles are of different devices: /device:TPU:1 before, /device:TPU:65 now
where the time goes in v5:
time: 110 us
  Pallas kernels  110 us (100%)
    pallas_call x1, Pallas kernels, local(): pl.pallas_call(functools.partial(main_kernel, lat_count, nx, nz), out_sha...  108 us

profile of v5, /device:TPU:65, one launch (start us, length us, event | category | flops | bytes accessed | tf_op | source)
XLA Modules:
  0.0 110.2 jit_solution(16925894758563079026)
XLA Ops:
  0.6 107.7 %block.1 = (bf16[2,4,64,512]{3,2,1,0:T(8,128)(2,1)}, bf16[2,32,512]{2,1,0:T(8,128)(2,1)}, f32[8,1,192]{2,1,0:T(1,128)}, f32[32,128]{1,0:T(8,128)}) custom-call(bf16[2,4,64,512]{3,2,1,0:T(8,128)(2,1)} %fields.1, s32[2,64]{1,0:T(2,128)} %classes.1, bf16[8,512]{1,0:T(8,128)(2,1)} %class_table.1, f32[1,512]{1,0:T(1,128)} %bitcast.16, bf16[192,512]{1,0:T(8,128)(2,1)} %bitcast.12, ...), custom_call_target="tpu_custom_call" | custom-call | tf_op jit(solution)/shard_map/block/pallas_call | solution.py:1076
  108.3 1.9 %hand_over.1 = (bf16[2,4,64,512]{3,2,1,0:T(8,128)(2,1)}, bf16[2,32,512]{2,1,0:T(8,128)(2,1)}, f32[8,1,192]{2,1,0:T(1,128)}, f32[32,128]{1,0:T(8,128)}) custom-call(bf16[2,4,64,512]{3,2,1,0:T(8,128)(2,1)} %get-tuple-element.12.refs_0_, bf16[2,32,512]{2,1,0:T(8,128)(2,1)} %get-tuple-element.13.refs_1_, f32[8,1,192]{2,1,0:T(1,128)} %get-tuple-element.14.refs_2_, ...), custom_call_target="tpu_custom_call" | custom-call | tf_op jit(solution)/shard_map/hand_over/pallas_call | solution.py:1106

commit v6 on v5

--- a/solution.py
+++ b/solution.py
@@ -859,7 +859,6 @@
     swap_mix.wait_recv()
     mix_all[aligned(far_half, HALF)] = mix_came[...].astype(F32)
     gather_up.start()
-    merge_sum.start()
     both = mix_all[...]
     grad_mix_rows[0:ROW] = high_lanes(both).astype(BF16)
     grad_mix_rows[ROW : 2 * ROW] = high_lanes(pltpu.roll(both, 64, 1)).astype(BF16)
@@ -883,7 +882,7 @@
         back[r] = (far_a + far_b).astype(BF16)
         send_back[r].start()
         grad_other[r] = own_a + own_b
-    merge_sum.middle()
+    merge_sum.start()
     for made in send_back:
         made.wait_recv()
     for r in range(2):
@@ -905,6 +904,7 @@
     gather_up.forward()
     for part in gnorm:
         part.middle()
+    merge_sum.middle()
     fine_sum.middle()
 
     grad_mn = mnorm.finish()

time: 110 us -> 108 us (0.982)
  the two profiles are of different devices: /device:TPU:65 before, /device:TPU:1 now
where the time goes in v6:
time: 108 us; the launch traced here: 107 us
  Pallas kernels  107 us (99%)
    pallas_call x1, Pallas kernels, local(): pl.pallas_call(functools.partial(main_kernel, lat_count, nx, nz), out_sha...  105 us

profile of v6, /device:TPU:1, one launch (start us, length us, event | category | flops | bytes accessed | tf_op | source)
XLA Modules:
  0.0 107.5 jit_solution(5424465362381034048)
XLA Ops:
  0.6 104.9 %block.1 = (bf16[2,4,64,512]{3,2,1,0:T(8,128)(2,1)}, bf16[2,32,512]{2,1,0:T(8,128)(2,1)}, f32[8,1,192]{2,1,0:T(1,128)}, f32[32,128]{1,0:T(8,128)}) custom-call(bf16[2,4,64,512]{3,2,1,0:T(8,128)(2,1)} %fields.1, s32[2,64]{1,0:T(2,128)} %classes.1, bf16[8,512]{1,0:T(8,128)(2,1)} %class_table.1, f32[1,512]{1,0:T(1,128)} %bitcast.16, bf16[192,512]{1,0:T(8,128)(2,1)} %bitcast.12, ...), custom_call_target="tpu_custom_call" | custom-call | tf_op jit(solution)/shard_map/block/pallas_call | solution.py:1076
  105.6 1.9 %hand_over.1 = (bf16[2,4,64,512]{3,2,1,0:T(8,128)(2,1)}, bf16[2,32,512]{2,1,0:T(8,128)(2,1)}, f32[8,1,192]{2,1,0:T(1,128)}, f32[32,128]{1,0:T(8,128)}) custom-call(bf16[2,4,64,512]{3,2,1,0:T(8,128)(2,1)} %get-tuple-element.12.refs_0_, bf16[2,32,512]{2,1,0:T(8,128)(2,1)} %get-tuple-element.13.refs_1_, f32[8,1,192]{2,1,0:T(1,128)} %get-tuple-element.14.refs_2_, ...), custom_call_target="tpu_custom_call" | custom-call | tf_op jit(solution)/shard_map/hand_over/pallas_call | solution.py:1106

commit v7 on v6

--- a/solution.py
+++ b/solution.py
@@ -648,7 +648,6 @@
     far.start()
     for made in send_keys:
         made.start()
-    gather_w.start()
 
     got_cotangent.wait()
     got_up.wait()
@@ -662,8 +661,9 @@
     quad = get(cotf, pl.ds(lax.div(kind, 2) * ROW + lax.rem(kind, 2), CTOK, stride=2))
     quad = jnp.where(lax.rem(tp, 2) == 0, quad[:, 0:256], quad[:, 256:512]).astype(BF16)
     lift_terms[...] = dot_nt(quad, up_weight[...]).astype(BF16).reshape(ZH, YS, CSHARE, DC)
+    gather_w.start()
+    far.pass_z()
     lift.start()
-    far.pass_z()
 
     for made in send_keys:
         made.wait_recv()

time: 108 us -> 109 us (level)
    pallas_call x1, Pallas kernels: 105 us -> 106 us  [local(): pl.pallas_call(functools.partial(main_kernel, lat_count, nx, nz), out_sha...]
where the time goes in v7:
time: 109 us
  Pallas kernels  108 us (99%)
    pallas_call x1, Pallas kernels, local(): pl.pallas_call(functools.partial(main_kernel, lat_count, nx, nz), out_sha...  106 us

profile of v7, /device:TPU:1, one launch (start us, length us, event | category | flops | bytes accessed | tf_op | source)
XLA Modules:
  0.0 108.6 jit_solution(15466432031478991722)
XLA Ops:
  0.6 106.1 %block.1 = (bf16[2,4,64,512]{3,2,1,0:T(8,128)(2,1)}, bf16[2,32,512]{2,1,0:T(8,128)(2,1)}, f32[8,1,192]{2,1,0:T(1,128)}, f32[32,128]{1,0:T(8,128)}) custom-call(bf16[2,4,64,512]{3,2,1,0:T(8,128)(2,1)} %fields.1, s32[2,64]{1,0:T(2,128)} %classes.1, bf16[8,512]{1,0:T(8,128)(2,1)} %class_table.1, f32[1,512]{1,0:T(1,128)} %bitcast.16, bf16[192,512]{1,0:T(8,128)(2,1)} %bitcast.12, ...), custom_call_target="tpu_custom_call" | custom-call | tf_op jit(solution)/shard_map/block/pallas_call | solution.py:1076
  106.7 1.9 %hand_over.1 = (bf16[2,4,64,512]{3,2,1,0:T(8,128)(2,1)}, bf16[2,32,512]{2,1,0:T(8,128)(2,1)}, f32[8,1,192]{2,1,0:T(1,128)}, f32[32,128]{1,0:T(8,128)}) custom-call(bf16[2,4,64,512]{3,2,1,0:T(8,128)(2,1)} %get-tuple-element.12.refs_0_, bf16[2,32,512]{2,1,0:T(8,128)(2,1)} %get-tuple-element.13.refs_1_, f32[8,1,192]{2,1,0:T(1,128)} %get-tuple-element.14.refs_2_, ...), custom_call_target="tpu_custom_call" | custom-call | tf_op jit(solution)/shard_map/hand_over/pallas_call | solution.py:1106
